TPU v7x, 32 devices: a whole 2x2x4 slice. The times are simulated.
32 devices in a mesh: dp: 4 (over y, x), expert: 8 (over z, core).
Axes of the slice: x: 2, y: 2, z: 4, core: 2. Of those that a mesh axis runs over, the one named last changes fastest.
Arguments:
- x_rows: bfloat16 [4096, 1024], P(('dp', 'expert')), may hold values from -6 to 6
- expert_ids: int32 [4096, 1], P(('dp', 'expert')), may hold values from 0 to 7; in each aligned block of 128 rows (0 to 127, 128 to 255, ...) at most 32 rows name the same one
- gates: float32 [4096, 1], P(('dp', 'expert')), may hold values from 0.1 to 1
- cotangent: bfloat16 [4096, 1024], P(('dp', 'expert')), may hold values from -6 to 6
- w_gate: bfloat16 [8, 1024, 384], P('expert', 'dp'), may hold values from -0.1875 to 0.1875
- w_up: bfloat16 [8, 1024, 384], P('expert', 'dp'), may hold values from -0.1875 to 0.1875
- w_down: bfloat16 [8, 384, 1024], P('expert', None, 'dp'), may hold values from -0.3125 to 0.3125
Outputs:
- gated_out: bfloat16 [4096, 1024], P(('dp', 'expert'))
- input_grad: bfloat16 [4096, 1024], P(('dp', 'expert'))
- gate_grad: float32 [4096, 1], P(('dp', 'expert'))
- grad_gate: bfloat16 [8, 1024, 384], P('expert', 'dp')
- grad_up: bfloat16 [8, 1024, 384], P('expert', 'dp')
- grad_down: bfloat16 [8, 384, 1024], P('expert', None, 'dp')
Inputs may be any that keep to these rules, and one draw needn't show every extreme that they name: `expert_ids`: among the rows of one device each expert id occurs at most 32 times, and in some device's rows some expert occurs exactly 32 times.
All inputs are finite; a program needn't handle non-finite values.
Results may differ from a plain program's by a relative error of at most 0.009.
Values may be sent and summed in bfloat16 or wider, within the bound.
A program may use at most 64 MiB of HBM per device.

v0:
```python
import jax
import jax.numpy as jnp
from jax import lax
from jax.sharding import PartitionSpec as P


def expert_rows(rows_in, rows_scaled, proj_gate, proj_up, proj_down):
    gate_act = jnp.dot(rows_in, proj_gate, preferred_element_type=jnp.float32)
    up_act = jnp.dot(rows_in, proj_up, preferred_element_type=jnp.float32)
    sigma = jax.nn.sigmoid(gate_act)
    hidden = (gate_act * sigma * up_act).astype(jnp.bfloat16)
    result = jnp.dot(hidden, proj_down, preferred_element_type=jnp.float32).astype(jnp.bfloat16)
    backed = jnp.dot(rows_scaled, proj_down.T, preferred_element_type=jnp.float32)
    d_gate_act = (backed * up_act * sigma * (1.0 + gate_act * (1.0 - sigma))).astype(jnp.bfloat16)
    d_up_act = (backed * gate_act * sigma).astype(jnp.bfloat16)
    d_input = (
        jnp.dot(d_gate_act, proj_gate.T, preferred_element_type=jnp.float32)
        + jnp.dot(d_up_act, proj_up.T, preferred_element_type=jnp.float32)
    ).astype(jnp.bfloat16)
    grad_g = jnp.dot(rows_in.T, d_gate_act, preferred_element_type=jnp.float32)
    grad_u = jnp.dot(rows_in.T, d_up_act, preferred_element_type=jnp.float32)
    grad_d = jnp.dot(hidden.T, rows_scaled, preferred_element_type=jnp.float32)
    return (result, d_input, (grad_g, grad_u, grad_d), (hidden, d_gate_act, d_up_act))


def rounded_sum(total, term):
    kept = lax.optimization_barrier(term.astype(jnp.bfloat16))
    return total + kept.astype(jnp.float32)


def per_device(x_rows, expert_ids, gates, cotangent, w_gate, w_up, w_down):
    full_gate, full_up, full_down = (
        lax.all_gather(w_gate, "dp", axis=1, tiled=True),
        lax.all_gather(w_up, "dp", axis=1, tiled=True),
        lax.all_gather(w_down, "dp", axis=2, tiled=True),
    )
    proj_gate = full_gate[0]
    proj_up = full_up[0]
    proj_down = full_down[0]
    experts = lax.axis_size("expert")
    row_count = x_rows.shape[0]
    width = x_rows.shape[1]
    capacity = 2 * row_count // experts
    row_ids = expert_ids[:, 0]
    onehot = (row_ids[:, None] == jnp.arange(experts, dtype=jnp.int32)[None, :]).astype(jnp.int32)
    ranking = jnp.sum((jnp.cumsum(onehot, 0) - onehot) * onehot, 1)
    slot = row_ids * capacity + ranking
    counts = jnp.sum(onehot, 0)
    scaled = (gates * cotangent.astype(jnp.float32)).astype(jnp.bfloat16)
    send_in = (
        jnp.zeros((experts * capacity, width), jnp.bfloat16)
        .at[slot]
        .set(x_rows)
        .reshape(experts, capacity, width)
    )
    send_scaled = (
        jnp.zeros((experts * capacity, width), jnp.bfloat16)
        .at[slot]
        .set(scaled)
        .reshape(experts, capacity, width)
    )
    recv_in, recv_scaled, recv_counts = (
        lax.all_to_all(send_in, "expert", split_axis=0, concat_axis=0, tiled=True),
        lax.all_to_all(send_scaled, "expert", split_axis=0, concat_axis=0, tiled=True),
        lax.all_to_all(
            counts.reshape(experts, 1), "expert", split_axis=0, concat_axis=0, tiled=True
        ),
    )
    flat_in = recv_in.reshape(experts * capacity, width)
    flat_scaled = recv_scaled.reshape(experts * capacity, width)
    slot_out, slot_grad, grads, acts = expert_rows(
        flat_in, flat_scaled, proj_gate, proj_up, proj_down
    )
    back_result, back_input = (
        lax.all_to_all(
            slot_out.reshape(experts, capacity, width),
            "expert",
            split_axis=0,
            concat_axis=0,
            tiled=True,
        ),
        lax.all_to_all(
            slot_grad.reshape(experts, capacity, width),
            "expert",
            split_axis=0,
            concat_axis=0,
            tiled=True,
        ),
    )
    row_out = back_result.reshape(experts * capacity, width)[slot]
    input_grad = back_input.reshape(experts * capacity, width)[slot]
    gated_out = (gates * row_out.astype(jnp.float32)).astype(jnp.bfloat16)
    gate_grad = jnp.sum(
        cotangent.astype(jnp.float32) * row_out.astype(jnp.float32), 1, keepdims=True
    )
    groups = lax.axis_size("dp")
    rows_here = flat_in.shape[0]
    slice_in, slice_scaled = (
        lax.all_to_all(flat_in, "dp", split_axis=1, concat_axis=0, tiled=True),
        lax.all_to_all(flat_scaled, "dp", split_axis=1, concat_axis=0, tiled=True),
    )
    all_hidden, all_dgate, all_dup = (
        lax.all_gather(acts[0], "dp", axis=0, tiled=True),
        lax.all_gather(acts[1], "dp", axis=0, tiled=True),
        lax.all_gather(acts[2], "dp", axis=0, tiled=True),
    )
    quarter = slice_in.shape[1]
    hidden_units = all_hidden.shape[1]
    total_gate = jnp.zeros((quarter, hidden_units), jnp.float32)
    total_up = jnp.zeros((quarter, hidden_units), jnp.float32)
    total_down = jnp.zeros((hidden_units, quarter), jnp.float32)
    for group in range(groups):
        first_row = group * rows_here
        group_in = slice_in[first_row : first_row + rows_here]
        group_scaled = slice_scaled[first_row : first_row + rows_here]
        group_hidden = all_hidden[first_row : first_row + rows_here]
        group_dgate = all_dgate[first_row : first_row + rows_here]
        group_dup = all_dup[first_row : first_row + rows_here]
        total_gate = rounded_sum(
            total_gate, jnp.dot(group_in.T, group_dgate, preferred_element_type=jnp.float32)
        )
        total_up = rounded_sum(
            total_up, jnp.dot(group_in.T, group_dup, preferred_element_type=jnp.float32)
        )
        total_down = rounded_sum(
            total_down, jnp.dot(group_hidden.T, group_scaled, preferred_element_type=jnp.float32)
        )
    summed_gate = total_gate[None]
    summed_up = total_up[None]
    summed_down = total_down[None]
    return (
        gated_out,
        input_grad,
        gate_grad,
        summed_gate.astype(jnp.bfloat16),
        summed_up.astype(jnp.bfloat16),
        summed_down.astype(jnp.bfloat16),
    )


def solution(mesh):
    in_specs = (
        P(("dp", "expert"), None),
        P(("dp", "expert"), None),
        P(("dp", "expert"), None),
        P(("dp", "expert"), None),
        P("expert", "dp", None),
        P("expert", "dp", None),
        P("expert", None, "dp"),
    )
    out_specs = (
        P(("dp", "expert"), None),
        P(("dp", "expert"), None),
        P(("dp", "expert"), None),
        P("expert", "dp", None),
        P("expert", "dp", None),
        P("expert", None, "dp"),
    )
    return jax.shard_map(
        per_device, mesh=mesh, in_specs=in_specs, out_specs=out_specs, check_vma=False
    )
```

profile of v0, /device:TPU:0, one launch (start us, length us, event | category | flops | bytes accessed | tf_op | source)
XLA Modules:
  0.0 165.4 jit_solution(11584780374851223283)
XLA Ops:
  1.7 2.4 %scatter_custom_fusion = bf16[256,1024]{1,0:T(8,128)(2,1)} fusion(s32[128]{0:T(128)S(1)} %fusion.36, bf16[128,1024]{1,0:T(8,128)(2,1)} %param.7, bf16[]{:T(256)} %constant.6.clone.1), kind=kCustom, calls=%fused_computation.44 | custom fusion | bytes 524800 | tf_op jit(solution)/shard_map/scatter | solution.py:53
  4.1 6.5 %all-to-all-start = ((bf16[8,32,1024]{2,1,0:T(8,128)(2,1)}), bf16[8,32,1024]{2,1,0:T(8,128)(2,1)S(1)}, u32[]{:S(2)}, u32[]{:S(2)}) async-start(bf16[8,32,1024]{2,1,0:T(8,128)(2,1)} %bitcast.4), calls=%async_computation | async-start | bytes 1048576 | tf_op jit(solution)/shard_map/all_to_all | solution.py:63
  11.2 2.0 %scatter_custom_fusion.1 = bf16[256,1024]{1,0:T(8,128)(2,1)} fusion(s32[128]{0:T(128)S(1)} %fusion.36, bf16[128,1024]{1,0:T(8,128)(2,1)S(1)} %copy-done.4, bf16[]{:T(256)} %constant.6.clone.1, f32[128]{0:T(128)S(1)} %bitcast.87), kind=kCustom, calls=%fused_computation.42 | custom fusion | flops 393216 | bytes 786946 | tf_op jit(solution)/shard_map/scatter | solution.py:59
  13.3 12.8 %all_gather.18 = bf16[1,1024,384]{2,1,0:T(8,128)(2,1)S(1)} all-gather(bf16[1,256,384]{2,1,0:T(8,128)(2,1)S(1)} %copy-done.9), channel_id=1, replica_groups=mesh['dp'=4,'expert'=8] {'dp'}, dimensions={1}, use_global_device_ids=true | all-gather | bytes 983040 | tf_op jit(solution)/shard_map/all_gather | solution.py:33
  26.1 4.5 %all-to-all-start.2 = ((bf16[8,32,1024]{2,1,0:T(8,128)(2,1)}), bf16[8,32,1024]{2,1,0:T(8,128)(2,1)S(1)}, u32[]{:S(2)}, u32[]{:S(2)}) async-start(bf16[8,32,1024]{2,1,0:T(8,128)(2,1)} %bitcast.11), calls=%async_computation.2 | async-start | bytes 1048576 | tf_op jit(solution)/shard_map/all_to_all | solution.py:64
  30.6 12.9 %all_gather.19 = bf16[1,1024,384]{2,1,0:T(8,128)(2,1)S(1)} all-gather(bf16[1,256,384]{2,1,0:T(8,128)(2,1)S(1)} %copy-done.10), channel_id=1, replica_groups=mesh['dp'=4,'expert'=8] {'dp'}, dimensions={1}, use_global_device_ids=true | all-gather | bytes 983040 | tf_op jit(solution)/shard_map/all_gather | solution.py:34
  43.6 15.3 %all_gather.20 = bf16[1,384,1024]{2,1,0:T(8,128)(2,1)S(1)} all-gather(bf16[1,384,256]{2,1,0:T(8,128)(2,1)S(1)} %copy-done.11), channel_id=1, replica_groups=mesh['dp'=4,'expert'=8] {'dp'}, dimensions={2}, use_global_device_ids=true | all-gather | bytes 983040 | tf_op jit(solution)/shard_map/all_gather | solution.py:35
  61.3 2.5 %multiply_convert_fusion = (bf16[256,384]{1,0:T(8,128)(2,1)}, bf16[256,384]{1,0:T(8,128)(2,1)S(1)}, bf16[256,384]{1,0:T(8,128)(2,1)S(1)}) fusion(f32[256,384]{1,0:T(8,128)} %fusion.9, f32[256,384]{1,0:T(8,128)} %fusion.5, bf16[256,1024]{1,0:T(8,128)(2,1)S(1)} %bitcast.80, bf16[1,384,1024]{2,1,0:T(8,128)(2,1)S(1)} %all_gather.20), kind=kOutput, calls=%fused_computation.38 | convolution fusion | flops 202899456 | bytes 2686976 | tf_op jit(solution)/shard_map/dot_general | solution.py:13
  64.3 12.8 %all_gather.21 = bf16[1024,384]{1,0:T(8,128)(2,1)} all-gather(bf16[256,384]{1,0:T(8,128)(2,1)S(1)} %get-tuple-element.7), channel_id=1, replica_groups=mesh['dp'=4,'expert'=8] {'dp'}, dimensions={0}, use_global_device_ids=true | all-gather | bytes 983040 | tf_op jit(solution)/shard_map/all_gather | solution.py:104
  78.3 11.1 %all_gather.23 = bf16[1024,384]{1,0:T(8,128)(2,1)} all-gather(bf16[256,384]{1,0:T(8,128)(2,1)S(1)} %get-tuple-element.8), channel_id=1, replica_groups=mesh['dp'=4,'expert'=8] {'dp'}, dimensions={0}, use_global_device_ids=true | all-gather | bytes 983040 | tf_op jit(solution)/shard_map/all_gather | solution.py:103
  90.6 4.3 %all-to-all-start.4 = ((bf16[256,4,256]{2,0,1:T(8,128)(2,1)}), bf16[256,4,256]{2,0,1:T(8,128)(2,1)}, u32[]{:S(2)}, u32[]{:S(2)}) async-start(bf16[256,4,256]{2,0,1:T(8,128)(2,1)} %copy.13), calls=%async_computation.4 | async-start | bytes 1048576 | tf_op jit(solution)/shard_map/all_to_all | solution.py:99
  96.3 12.3 %all_gather.22 = bf16[1024,384]{1,0:T(8,128)(2,1)S(1)} all-gather(bf16[256,384]{1,0:T(8,128)(2,1)S(1)} %copy-done.8), channel_id=1, replica_groups=mesh['dp'=4,'expert'=8] {'dp'}, dimensions={0}, use_global_device_ids=true | all-gather | bytes 983040 | tf_op jit(solution)/shard_map/all_gather | solution.py:105
  109.8 3.6 %all-to-all-start.5 = ((bf16[256,4,256]{2,0,1:T(8,128)(2,1)}), bf16[256,4,256]{2,0,1:T(8,128)(2,1)S(1)}, u32[]{:S(2)}, u32[]{:S(2)}) async-start(bf16[256,4,256]{2,0,1:T(8,128)(2,1)} %copy.14), calls=%async_computation.5 | async-start | bytes 1048576 | tf_op jit(solution)/shard_map/all_to_all | solution.py:100
  117.0 1.8 %convolution_convert_fusion.12 = bf16[256,384]{1,0:T(8,128)(2,1)} fusion(bf16[1024,384]{1,0:T(8,128)(2,1)S(1)} %copy-done.7, bf16[4,256,256]{2,1,0:T(8,128)(2,1)} %bitcast.16), kind=kOutput, calls=%fused_computation.18 | convolution fusion | flops 50429952 | bytes 524288 | tf_op jit(solution)/shard_map/dot_general | solution.py:120
  118.8 1.8 %convolution_convert_fusion.5 = bf16[256,384]{1,0:T(8,128)(2,1)} fusion(bf16[1024,384]{1,0:T(8,128)(2,1)S(1)} %all_gather.22, bf16[4,256,256]{2,1,0:T(8,128)(2,1)} %bitcast.16), kind=kOutput, calls=%fused_computation.11 | convolution fusion | flops 50429952 | bytes 524288 | tf_op jit(solution)/shard_map/dot_general | solution.py:123
  120.6 1.8 %convolution_convert_fusion.6 = bf16[256,384]{1,0:T(8,128)(2,1)} fusion(bf16[1024,384]{1,0:T(8,128)(2,1)S(1)} %all_gather.22, bf16[4,256,256]{2,1,0:T(8,128)(2,1)} %bitcast.16), kind=kOutput, calls=%fused_computation.12 | convolution fusion | flops 50429952 | bytes 524288 | tf_op jit(solution)/shard_map/dot_general | solution.py:123
  122.4 1.8 %convolution_convert_fusion.7 = bf16[256,384]{1,0:T(8,128)(2,1)} fusion(bf16[1024,384]{1,0:T(8,128)(2,1)S(1)} %all_gather.22, bf16[4,256,256]{2,1,0:T(8,128)(2,1)} %bitcast.16), kind=kOutput, calls=%fused_computation.13 | convolution fusion | flops 50429952 | bytes 524288 | tf_op jit(solution)/shard_map/dot_general | solution.py:123
  124.3 1.9 %convolution_convert_fusion.8 = bf16[256,384]{1,0:T(8,128)(2,1)} fusion(bf16[1024,384]{1,0:T(8,128)(2,1)S(1)} %all_gather.22, bf16[4,256,256]{2,1,0:T(8,128)(2,1)} %bitcast.16), kind=kOutput, calls=%fused_computation.14 | convolution fusion | flops 50429952 | bytes 524288 | tf_op jit(solution)/shard_map/dot_general | solution.py:123
  126.2 3.5 %all-to-all-start.1 = ((bf16[8,32,1024]{2,1,0:T(8,128)(2,1)}), bf16[8,32,1024]{2,1,0:T(8,128)(2,1)S(1)}, u32[]{:S(2)}, u32[]{:S(2)}) async-start(bf16[8,32,1024]{2,1,0:T(8,128)(2,1)} %bitcast.9), calls=%async_computation.1 | async-start | bytes 1048576 | tf_op jit(solution)/shard_map/all_to_all | solution.py:75
  133.5 11.5 %all-to-all-done.1 = bf16[8,32,1024]{2,1,0:T(8,128)(2,1)S(1)} async-done(((bf16[8,32,1024]{2,1,0:T(8,128)(2,1)}), bf16[8,32,1024]{2,1,0:T(8,128)(2,1)S(1)}, u32[]{:S(2)}, u32[]{:S(2)}) %all-to-all-start.1) | async-done | bytes 524320 | tf_op jit(solution)/shard_map/all_to_all | solution.py:75
  145.0 3.6 %all-to-all-start.3 = ((bf16[8,32,1024]{2,1,0:T(8,128)(2,1)}), bf16[8,32,1024]{2,1,0:T(8,128)(2,1)S(1)}, u32[]{:S(2)}, u32[]{:S(2)}) async-start(bf16[8,32,1024]{2,1,0:T(8,128)(2,1)} %bitcast.13), calls=%async_computation.3 | async-start | bytes 1048576 | tf_op jit(solution)/shard_map/all_to_all | solution.py:82
  152.9 1.3 fusion.13
  154.3 9.6 %all-to-all-done.3 = bf16[8,32,1024]{2,1,0:T(8,128)(2,1)S(1)} async-done(((bf16[8,32,1024]{2,1,0:T(8,128)(2,1)}), bf16[8,32,1024]{2,1,0:T(8,128)(2,1)S(1)}, u32[]{:S(2)}, u32[]{:S(2)}) %all-to-all-start.3) | async-done | bytes 524320 | tf_op jit(solution)/shard_map/all_to_all | solution.py:82
  163.9 1.6 gather_fusion.1
  (75 shorter events, 21.2 us)
Async XLA Ops:
  4.1 6.5 %copy-start.4 = (bf16[128,1024]{1,0:T(8,128)(2,1)S(1)}, bf16[128,1024]{1,0:T(8,128)(2,1)}, u32[]{:S(2)}) copy-start(bf16[128,1024]{1,0:T(8,128)(2,1)} %param.10) | copy-start | bytes 786436
  4.1 22.0 %all-to-all-start = ((bf16[8,32,1024]{2,1,0:T(8,128)(2,1)}), bf16[8,32,1024]{2,1,0:T(8,128)(2,1)S(1)}, u32[]{:S(2)}, u32[]{:S(2)}) async-start(bf16[8,32,1024]{2,1,0:T(8,128)(2,1)} %bitcast.4), calls=%async_computation | async-start | bytes 1048576 | tf_op jit(solution)/shard_map/all_to_all | solution.py:63
  11.2 2.0 %copy-start.9 = (bf16[1,256,384]{2,1,0:T(8,128)(2,1)S(1)}, bf16[1,256,384]{2,1,0:T(8,128)(2,1)}, u32[]{:S(2)}) copy-start(bf16[1,256,384]{2,1,0:T(8,128)(2,1)} %param.11) | copy-start | bytes 589828
  26.1 4.5 %copy-start.10 = (bf16[1,256,384]{2,1,0:T(8,128)(2,1)S(1)}, bf16[1,256,384]{2,1,0:T(8,128)(2,1)}, u32[]{:S(2)}) copy-start(bf16[1,256,384]{2,1,0:T(8,128)(2,1)} %param.12) | copy-start | bytes 589828
  26.1 35.2 %all-to-all-start.2 = ((bf16[8,32,1024]{2,1,0:T(8,128)(2,1)}), bf16[8,32,1024]{2,1,0:T(8,128)(2,1)S(1)}, u32[]{:S(2)}, u32[]{:S(2)}) async-start(bf16[8,32,1024]{2,1,0:T(8,128)(2,1)} %bitcast.11), calls=%async_computation.2 | async-start | bytes 1048576 | tf_op jit(solution)/shard_map/all_to_all | solution.py:64
  30.6 13.0 %copy-start.11 = (bf16[1,384,256]{2,1,0:T(8,128)(2,1)S(1)}, bf16[1,384,256]{2,1,0:T(8,128)(2,1)}, u32[]{:S(2)}) copy-start(bf16[1,384,256]{2,1,0:T(8,128)(2,1)} %param.13) | copy-start | bytes 589828
  58.9 2.4 %copy-start = (bf16[1,384,1024]{2,1,0:T(8,128)(2,1)}, bf16[1,384,1024]{2,1,0:T(8,128)(2,1)S(1)}, u32[]{:S(2)}) copy-start(bf16[1,384,1024]{2,1,0:T(8,128)(2,1)S(1)} %all_gather.20) | copy-start | bytes 2359300
  61.3 2.5 %copy-start.2 = (bf16[8,32,1024]{2,1,0:T(8,128)(2,1)}, bf16[8,32,1024]{2,1,0:T(8,128)(2,1)S(1)}, u32[]{:S(2)}) copy-start(bf16[8,32,1024]{2,1,0:T(8,128)(2,1)S(1)} %all-to-all-done.2) | copy-start | bytes 1572868
  64.3 12.8 %copy-start.1 = (bf16[1,384,1024]{2,1,0:T(8,128)(2,1)S(1)}, bf16[1,384,1024]{2,1,0:T(8,128)(2,1)}, u32[]{:S(2)}) copy-start(bf16[1,384,1024]{2,1,0:T(8,128)(2,1)} %copy-done) | copy-start | bytes 2359300
  90.6 4.3 %copy-start.3 = (bf16[8,32,1024]{2,1,0:T(8,128)(2,1)S(1)}, bf16[8,32,1024]{2,1,0:T(8,128)(2,1)}, u32[]{:S(2)}) copy-start(bf16[8,32,1024]{2,1,0:T(8,128)(2,1)} %copy-done.2) | copy-start | bytes 1572868
  90.6 19.2 %all-to-all-start.4 = ((bf16[256,4,256]{2,0,1:T(8,128)(2,1)}), bf16[256,4,256]{2,0,1:T(8,128)(2,1)}, u32[]{:S(2)}, u32[]{:S(2)}) async-start(bf16[256,4,256]{2,0,1:T(8,128)(2,1)} %copy.13), calls=%async_computation.4 | async-start | bytes 1048576 | tf_op jit(solution)/shard_map/all_to_all | solution.py:99
  109.8 3.6 %copy-start.7 = (bf16[1024,384]{1,0:T(8,128)(2,1)S(1)}, bf16[1024,384]{1,0:T(8,128)(2,1)}, u32[]{:S(2)}) copy-start(bf16[1024,384]{1,0:T(8,128)(2,1)} %all_gather.21) | copy-start | bytes 2359300
  109.8 16.3 %all-to-all-start.5 = ((bf16[256,4,256]{2,0,1:T(8,128)(2,1)}), bf16[256,4,256]{2,0,1:T(8,128)(2,1)S(1)}, u32[]{:S(2)}, u32[]{:S(2)}) async-start(bf16[256,4,256]{2,0,1:T(8,128)(2,1)} %copy.14), calls=%async_computation.5 | async-start | bytes 1048576 | tf_op jit(solution)/shard_map/all_to_all | solution.py:100
  124.3 5.4 %copy-start.6 = (bf16[1024,384]{1,0:T(8,128)(2,1)S(1)}, bf16[1024,384]{1,0:T(8,128)(2,1)}, u32[]{:S(2)}) copy-start(bf16[1024,384]{1,0:T(8,128)(2,1)} %all_gather.23) | copy-start | bytes 2359300
  126.2 18.8 %all-to-all-start.1 = ((bf16[8,32,1024]{2,1,0:T(8,128)(2,1)}), bf16[8,32,1024]{2,1,0:T(8,128)(2,1)S(1)}, u32[]{:S(2)}, u32[]{:S(2)}) async-start(bf16[8,32,1024]{2,1,0:T(8,128)(2,1)} %bitcast.9), calls=%async_computation.1 | async-start | bytes 1048576 | tf_op jit(solution)/shard_map/all_to_all | solution.py:75
  145.0 3.6 %copy-start.12 = (bf16[256,384]{1,0:T(8,128)(2,1)S(1)}, bf16[256,384]{1,0:T(8,128)(2,1)}, u32[]{:S(2)}) copy-start(bf16[256,384]{1,0:T(8,128)(2,1)} %convolution_convert_fusion.12) | copy-start | bytes 589828
  145.0 18.9 %all-to-all-start.3 = ((bf16[8,32,1024]{2,1,0:T(8,128)(2,1)}), bf16[8,32,1024]{2,1,0:T(8,128)(2,1)S(1)}, u32[]{:S(2)}, u32[]{:S(2)}) async-start(bf16[8,32,1024]{2,1,0:T(8,128)(2,1)} %bitcast.13), calls=%async_computation.3 | async-start | bytes 1048576 | tf_op jit(solution)/shard_map/all_to_all | solution.py:82
  148.6 1.1 copy-start.14
  148.6 1.2 copy-start.15
  148.7 1.3 copy-start.16
  149.9 1.1 copy-start.18
  149.9 1.2 copy-start.19
  149.9 1.3 copy-start.20
  152.0 0.9 copy-start.5
  (5 other events, 4.1 us)
where the time goes:
time: 167 us; the launch traced here: 165 us
  blocking collectives  77.3 us (46%)
  starting transfers between devices  25.9 us (16%)
  matrix products  24.3 us (15%)
  waiting for transfers between devices  21.1 us (13%)
  local copies, waits for them, and re-layouts  9.76 us (6%)
  other arithmetic  6.15 us (4%)
    all_gather x1, blocking collectives, per_device(): lax.all_gather(w_down, 'dp', axis=2, tiled=True)  15.3 us
    all_gather x1, blocking collectives, per_device(): lax.all_gather(w_up, 'dp', axis=1, tiled=True)  12.9 us
    all_gather x1, blocking collectives, per_device(): lax.all_gather(w_gate, 'dp', axis=1, tiled=True)  12.8 us
    all_gather x1, blocking collectives, per_device(): lax.all_gather(acts[1], 'dp', axis=0, tiled=True)  12.8 us
    all_gather x1, blocking collectives, per_device(): lax.all_gather(acts[2], 'dp', axis=0, tiled=True)  12.3 us
    all_to_all x1, waiting for transfers between devices, per_device(): lax.all_to_all(slot_out.reshape(experts, capacity, width), 'expert', spli...  11.5 us
    all_gather x1, blocking collectives, per_device(): lax.all_gather(acts[0], 'dp', axis=0, tiled=True)  11.1 us
    all_to_all x1, waiting for transfers between devices, per_device(): lax.all_to_all(slot_grad.reshape(experts, capacity, width), 'expert', spl...  9.61 us
  transfers between devices with their start and end apart: 6, of which 2 were waited for; matrix products, arithmetic and copies ran while one was open for 17% of the time, Pallas kernels for 0%

commit v1 on v0

--- a/solution.py
+++ b/solution.py
@@ -1,6 +1,10 @@
+import functools
+
 import jax
 import jax.numpy as jnp
 from jax import lax
+from jax.experimental import pallas as pl
+from jax.experimental.pallas import tpu as pltpu
 from jax.sharding import PartitionSpec as P
 
 
@@ -28,7 +32,7 @@
     return total + kept.astype(jnp.float32)
 
 
-def per_device(x_rows, expert_ids, gates, cotangent, w_gate, w_up, w_down):
+def collective_device(x_rows, expert_ids, gates, cotangent, w_gate, w_up, w_down):
     full_gate, full_up, full_down = (
         lax.all_gather(w_gate, "dp", axis=1, tiled=True),
         lax.all_gather(w_up, "dp", axis=1, tiled=True),
@@ -138,6 +142,237 @@
     )
 
 
+F32 = jnp.float32
+BF16 = jnp.bfloat16
+
+
+def dot(a, b):
+    return lax.dot_general(a, b, (((1,), (0,)), ((), ())), preferred_element_type=F32)
+
+
+def dot_left_t(a, b):
+    return lax.dot_general(a, b, (((0,), (0,)), ((), ())), preferred_element_type=F32)
+
+
+def dot_right_t(a, b):
+    return lax.dot_general(a, b, (((1,), (1,)), ((), ())), preferred_element_type=F32)
+
+
+def flipped(index, bits, size):
+    result, place = 0, 1
+    while place < size:
+        digit = (index // place) % 2
+        result = result + ((digit + 1) % 2 if bits & place else digit) * place
+        place *= 2
+    return result
+
+
+def layer_kernel(
+    n_dp, n_ex, cap,
+    x_ref, ids_ref, gates_ref, cot_ref, wg_ref, wu_ref, wd_ref,
+    gated_ref, igrad_ref, ggrad_ref, ogg_ref, ogu_ref, ogd_ref,
+    place_ref, send_x, send_s, recv_x, recv_s, out_send, in_send, out_back, in_back,
+    full_g, full_u, full_d, hid_ref, fac_g, fac_u, dg_ref, du_ref,
+    part_g, part_u, part_d, got_g, got_u, got_d,
+    z_send, z_recv, w_send, w_recv, g_send, g_recv,
+):
+    me_e, me_d = lax.axis_index("expert"), lax.axis_index("dp")
+    z_peers = [(k, flipped(me_e, k, n_ex)) for k in range(n_ex - 1, 0, -1)]
+    d_peers = [(k, flipped(me_d, k, n_dp)) for k in range(n_dp - 1, 0, -1)]
+    width = x_ref.shape[1]
+    piece = width // n_dp
+
+    barrier = pltpu.get_barrier_semaphore()
+    for _, peer in z_peers:
+        pl.semaphore_signal(barrier, inc=1, device_id={"expert": peer}, device_id_type=pl.DeviceIdType.MESH)
+    for _, peer in d_peers:
+        pl.semaphore_signal(barrier, inc=1, device_id={"dp": peer}, device_id_type=pl.DeviceIdType.MESH)
+
+    def slots(index):
+        return pl.ds(pl.multiple_of(index * cap, cap), cap)
+
+    def columns(q):
+        return slice(q * piece, (q + 1) * piece)
+
+    rows = x_ref.shape[0]
+    onehot = (ids_ref[...] == lax.broadcasted_iota(jnp.int32, (rows, n_ex), 1)).astype(F32)
+    earlier = (
+        lax.broadcasted_iota(jnp.int32, (rows, rows), 0) > lax.broadcasted_iota(jnp.int32, (rows, rows), 1)
+    ).astype(BF16)
+    ranks = jnp.sum(dot(earlier, onehot.astype(BF16)) * onehot, 1, keepdims=True)
+    slot = ids_ref[...] * cap + ranks.astype(jnp.int32)
+    place_ref[...] = (slot == lax.broadcasted_iota(jnp.int32, (rows, n_ex * cap), 1)).astype(BF16)
+    send_x[...] = dot_left_t(place_ref[...], x_ref[...]).astype(BF16)
+
+    pl.semaphore_wait(barrier, n_dp + n_ex - 2)
+
+    copies = []
+
+    def z_start(which, source, target):
+        made = []
+        for k, peer in z_peers:
+            copy = pltpu.make_async_remote_copy(
+                src_ref=source.at[slots(peer)],
+                dst_ref=target.at[slots(me_e)],
+                send_sem=z_send.at[which, k],
+                recv_sem=z_recv.at[which, k],
+                device_id={"expert": peer},
+                device_id_type=pl.DeviceIdType.MESH,
+            )
+            copy.start()
+            made.append(copy)
+        copies.extend(made)
+        target[slots(me_e), :] = source[slots(me_e), :]
+        return made
+
+    def w_start(which, source, target):
+        made = []
+        for k, peer in d_peers:
+            copy = pltpu.make_async_remote_copy(
+                src_ref=source.at[0],
+                dst_ref=target.at[me_d],
+                send_sem=w_send.at[which, k],
+                recv_sem=w_recv.at[which, k],
+                device_id={"dp": peer},
+                device_id_type=pl.DeviceIdType.MESH,
+            )
+            copy.start()
+            made.append(copy)
+        copies.extend(made)
+        target[me_d] = source[0]
+        return made
+
+    def g_start(which, source, target):
+        made = []
+        for k, peer in d_peers:
+            copy = pltpu.make_async_remote_copy(
+                src_ref=source.at[peer],
+                dst_ref=target.at[k],
+                send_sem=g_send.at[which, k],
+                recv_sem=g_recv.at[which, k],
+                device_id={"dp": peer},
+                device_id_type=pl.DeviceIdType.MESH,
+            )
+            copy.start()
+            made.append(copy)
+        copies.extend(made)
+        return made
+
+    def arrived(made):
+        for copy in made:
+            copy.wait_recv()
+
+    x_copies = z_start(0, send_x, recv_x)
+    g_copies = w_start(0, wg_ref, full_g)
+    u_copies = w_start(1, wu_ref, full_u)
+    d_copies = w_start(2, wd_ref, full_d)
+
+    scaled = (gates_ref[...] * cot_ref[...].astype(F32)).astype(BF16)
+    send_s[...] = dot_left_t(place_ref[...], scaled).astype(BF16)
+    s_copies = z_start(1, send_s, recv_s)
+
+    arrived(x_copies)
+    arrived(g_copies)
+    hidden_units = wg_ref.shape[2]
+    gate_act = dot(recv_x[...], full_g[...].reshape(width, hidden_units))
+    arrived(u_copies)
+    up_act = dot(recv_x[...], full_u[...].reshape(width, hidden_units))
+    sigma = jax.nn.sigmoid(gate_act)
+    hid_ref[...] = (gate_act * sigma * up_act).astype(BF16)
+    fac_g[...] = up_act * sigma * (1.0 + gate_act * (1.0 - sigma))
+    fac_u[...] = gate_act * sigma
+    arrived(d_copies)
+    for q in range(n_dp):
+        out_send[:, columns(q)] = dot(hid_ref[...], full_d[q]).astype(BF16)
+    out_copies = z_start(2, out_send, out_back)
+
+    arrived(s_copies)
+    for q in range(n_dp):
+        part_d[q] = dot_left_t(hid_ref[...], recv_s[:, columns(q)]).astype(BF16)
+    pd_copies = g_start(2, part_d, got_d)
+    backed = dot_right_t(recv_s[:, columns(0)], full_d[0])
+    for q in range(1, n_dp):
+        backed = backed + dot_right_t(recv_s[:, columns(q)], full_d[q])
+    dg_ref[...] = (backed * fac_g[...]).astype(BF16)
+    du_ref[...] = (backed * fac_u[...]).astype(BF16)
+    for q in range(n_dp):
+        part_g[q] = dot_left_t(recv_x[:, columns(q)], dg_ref[...]).astype(BF16)
+    pg_copies = g_start(0, part_g, got_g)
+    for q in range(n_dp):
+        part_u[q] = dot_left_t(recv_x[:, columns(q)], du_ref[...]).astype(BF16)
+    pu_copies = g_start(1, part_u, got_u)
+    for q in range(n_dp):
+        in_send[:, columns(q)] = (
+            dot_right_t(dg_ref[...], full_g[q]) + dot_right_t(du_ref[...], full_u[q])
+        ).astype(BF16)
+    in_copies = z_start(3, in_send, in_back)
+
+    arrived(out_copies)
+    row_out = dot(place_ref[...], out_back[...])
+    gated_ref[...] = (gates_ref[...] * row_out).astype(BF16)
+    ggrad_ref[...] = jnp.sum(cot_ref[...].astype(F32) * row_out, 1, keepdims=True)
+    for made, part, got, out in (
+        (pd_copies, part_d, got_d, ogd_ref),
+        (pg_copies, part_g, got_g, ogg_ref),
+        (pu_copies, part_u, got_u, ogu_ref),
+    ):
+        arrived(made)
+        total = part[me_d].astype(F32)
+        for k in range(1, n_dp):
+            total = total + got[k].astype(F32)
+        out[0] = total.astype(BF16)
+    arrived(in_copies)
+    igrad_ref[...] = dot(place_ref[...], in_back[...]).astype(BF16)
+    for copy in copies:
+        copy.wait_send()
+
+
+def power_of_two(size):
+    return size & (size - 1) == 0
+
+
+def per_device(x_rows, expert_ids, gates, cotangent, w_gate, w_up, w_down):
+    n_dp, n_ex = lax.axis_size("dp"), lax.axis_size("expert")
+    rows, width = x_rows.shape
+    cap = 2 * rows // n_ex
+    _, piece, hidden = w_gate.shape
+    if cap % 16 or not power_of_two(n_ex) or not power_of_two(n_dp):
+        return collective_device(x_rows, expert_ids, gates, cotangent, w_gate, w_up, w_down)
+    total = n_ex * cap
+    vmem = pl.BlockSpec(memory_space=pltpu.VMEM)
+    slots_of = pltpu.VMEM((total, width), BF16)
+    gates_of = pltpu.VMEM((n_dp, piece, hidden), BF16)
+    downs_of = pltpu.VMEM((n_dp, hidden, piece), BF16)
+    acts_of = pltpu.VMEM((total, hidden), BF16)
+    facs_of = pltpu.VMEM((total, hidden), F32)
+    return pl.pallas_call(
+        functools.partial(layer_kernel, n_dp, n_ex, cap),
+        out_shape=(
+            jax.ShapeDtypeStruct((rows, width), BF16),
+            jax.ShapeDtypeStruct((rows, width), BF16),
+            jax.ShapeDtypeStruct((rows, 1), F32),
+            jax.ShapeDtypeStruct(w_gate.shape, BF16),
+            jax.ShapeDtypeStruct(w_up.shape, BF16),
+            jax.ShapeDtypeStruct(w_down.shape, BF16),
+        ),
+        in_specs=[vmem] * 7,
+        out_specs=[vmem] * 6,
+        scratch_shapes=[
+            pltpu.VMEM((rows, total), BF16),
+            slots_of, slots_of, slots_of, slots_of, slots_of, slots_of, slots_of, slots_of,
+            gates_of, gates_of, downs_of,
+            acts_of, facs_of, facs_of, acts_of, acts_of,
+            gates_of, gates_of, downs_of, gates_of, gates_of, downs_of,
+            pltpu.SemaphoreType.DMA((4, n_ex)), pltpu.SemaphoreType.DMA((4, n_ex)),
+            pltpu.SemaphoreType.DMA((3, n_dp)), pltpu.SemaphoreType.DMA((3, n_dp)),
+            pltpu.SemaphoreType.DMA((3, n_dp)), pltpu.SemaphoreType.DMA((3, n_dp)),
+        ],
+        compiler_params=pltpu.CompilerParams(
+            collective_id=0, has_side_effects=True, vmem_limit_bytes=40 * 1024 * 1024
+        ),
+    )(x_rows, expert_ids, gates, cotangent, w_gate, w_up, w_down)
+
+
 def solution(mesh):
     in_specs = (
         P(("dp", "expert"), None),

time: 167 us -> 73.4 us (0.44)
  blocking collectives: 77.3 us -> 0 us
  Pallas kernels: 0 us -> 62.9 us
  starting transfers between devices: 25.9 us -> 0 us
  matrix products: 24.3 us -> 0 us
  waiting for transfers between devices: 21.1 us -> 0 us
  other arithmetic: 6.15 us -> 0 us
    all_gather x6 -> x0, blocking collectives: 77.3 us -> none  [the longest x1 15.3 us: per_device(): lax.all_gather(w_down, 'dp', axis=2, tiled=True)]
    pallas_call x0 -> x1, Pallas kernels: none -> 62.9 us  [per_device(): pl.pallas_call(functools.partial(layer_kernel, n_dp, n_ex, cap), out_shap...]
    all_to_all x6 -> x0, starting transfers between devices: 25.9 us -> none  [the longest x1 6.46 us: per_device(): lax.all_to_all(send_in, 'expert', split_axis=0, concat_axis=0, tiled=True)]
    dot_general x18 -> x0, matrix products: 24.3 us -> none  [the longest x4 7.4 us: per_device(): jnp.dot(group_in.T, group_dup, preferred_element_type=jnp.float32)]
    all_to_all x6 -> x0, waiting for transfers between devices: 21.1 us -> none  [the longest x1 11.5 us: per_device(): lax.all_to_all(slot_out.reshape(experts, capacity, width), 'expert', spli...]
    unnamed x46 -> x19, local copies, waits for them, and re-layouts: 2.46 us -> 8.99 us
    all_to_all x4 -> x0, local copies, waits for them, and re-layouts: 2.48 us -> none  [the longest x2 1.25 us: per_device(): lax.all_to_all(flat_scaled, 'dp', split_axis=1, concat_axis=0, tiled=True)]
    convert_element_type x4 -> x0, other arithmetic: 2.43 us -> none  [the longest x1 0.79 us: per_device(): summed_down.astype(jnp.bfloat16)]
  transfers between devices with their start and end apart: 6 -> 0, of which waited for: 2 -> 0; matrix products, arithmetic and copies ran while one was open for 17% -> 0% of each run, Pallas kernels for 0% -> 0%
where the time goes in v1:
time: 73.4 us; the launch traced here: 73.2 us
  Pallas kernels  62.9 us (86%)
  local copies, waits for them, and re-layouts  9.58 us (13%)
    pallas_call x1, Pallas kernels, per_device(): pl.pallas_call(functools.partial(layer_kernel, n_dp, n_ex, cap), out_shap...  62.9 us
    unnamed x19, local copies, waits for them, and re-layouts  8.99 us

profile of v1, /device:TPU:0, one launch (start us, length us, event | category | flops | bytes accessed | tf_op | source)
XLA Modules:
  0.0 73.2 jit_solution(10884363444398010024)
XLA Ops:
  0.6 0.0 copy-start.5
  0.6 0.8 %copy.13.ids_ref = s32[128,1]{1,0:T(8,128)S(1)} copy(s32[128,1]{0,1:T(1,128)} %param.8) | data formatting | bytes 1024 | tf_op args[1]
  1.4 0.0 copy-done.5
  1.4 0.1 copy.14.gates_ref
  1.5 0.0 copy-start
  1.5 0.9 %copy-done = bf16[128,1024]{1,0:T(8,128)(2,1)S(1)} copy-done((bf16[128,1024]{1,0:T(8,128)(2,1)S(1)}, bf16[128,1024]{1,0:T(8,128)(2,1)}, u32[]{:S(2)}) %copy-start) | copy-done | bytes 262168
  2.5 0.0 copy-start.1
  2.5 0.9 %copy-done.1 = bf16[128,1024]{1,0:T(8,128)(2,1)S(1)} copy-done((bf16[128,1024]{1,0:T(8,128)(2,1)S(1)}, bf16[128,1024]{1,0:T(8,128)(2,1)}, u32[]{:S(2)}) %copy-start.1) | copy-done | bytes 262168
  3.4 0.0 copy-start.2
  3.4 0.9 %copy-done.2 = bf16[1,256,384]{2,1,0:T(8,128)(2,1)S(1)} copy-done((bf16[1,256,384]{2,1,0:T(8,128)(2,1)S(1)}, bf16[1,256,384]{2,1,0:T(8,128)(2,1)}, u32[]{:S(2)}) %copy-start.2) | copy-done | bytes 196632
  4.4 0.0 copy-start.3
  4.4 0.9 %copy-done.3 = bf16[1,256,384]{2,1,0:T(8,128)(2,1)S(1)} copy-done((bf16[1,256,384]{2,1,0:T(8,128)(2,1)S(1)}, bf16[1,256,384]{2,1,0:T(8,128)(2,1)}, u32[]{:S(2)}) %copy-start.3) | copy-done | bytes 196632
  5.3 0.0 copy-start.4
  5.3 0.9 %copy-done.4 = bf16[1,384,256]{2,1,0:T(8,128)(2,1)S(1)} copy-done((bf16[1,384,256]{2,1,0:T(8,128)(2,1)S(1)}, bf16[1,384,256]{2,1,0:T(8,128)(2,1)}, u32[]{:S(2)}) %copy-start.4) | copy-done | bytes 196632
  6.2 62.9 %shard_map.118 = (bf16[128,1024]{1,0:T(8,128)(2,1)S(1)}, bf16[128,1024]{1,0:T(8,128)(2,1)S(1)}, f32[128,1]{1,0:T(8,128)S(1)}, bf16[1,256,384]{2,1,0:T(8,128)(2,1...) custom-call(bf16[128,1024]{1,0:T(8,128)(2,1)S(1)} %copy-done, s32[128,1]{1,0:T(8,128)S(1)} %copy.13.ids_ref, ...), custom_call_target="tpu_custom_call" | custom-call | tf_op jit(solution)/shard_map/pallas_call | solution.py:348
  69.2 0.6 copy.15
  69.7 0.7 copy.21
  70.4 0.7 copy.22
  71.1 0.7 copy.23
  71.8 0.7 copy.24
  72.5 0.7 copy.25
Async XLA Ops:
  0.6 0.8 %copy-start.5 = (f32[128,1]{0,1:T(1,128)S(1)}, f32[128,1]{0,1:T(1,128)}, u32[]{:S(2)}) copy-start(f32[128,1]{0,1:T(1,128)} %param.9) | copy-start | bytes 1540
  1.5 1.0 %copy-start = (bf16[128,1024]{1,0:T(8,128)(2,1)S(1)}, bf16[128,1024]{1,0:T(8,128)(2,1)}, u32[]{:S(2)}) copy-start(bf16[128,1024]{1,0:T(8,128)(2,1)} %x_ref.1) | copy-start | bytes 786436
  2.5 0.9 %copy-start.1 = (bf16[128,1024]{1,0:T(8,128)(2,1)S(1)}, bf16[128,1024]{1,0:T(8,128)(2,1)}, u32[]{:S(2)}) copy-start(bf16[128,1024]{1,0:T(8,128)(2,1)} %cot_ref.1) | copy-start | bytes 786436
  3.4 0.9 %copy-start.2 = (bf16[1,256,384]{2,1,0:T(8,128)(2,1)S(1)}, bf16[1,256,384]{2,1,0:T(8,128)(2,1)}, u32[]{:S(2)}) copy-start(bf16[1,256,384]{2,1,0:T(8,128)(2,1)} %wg_ref.1) | copy-start | bytes 589828
  4.4 0.9 %copy-start.3 = (bf16[1,256,384]{2,1,0:T(8,128)(2,1)S(1)}, bf16[1,256,384]{2,1,0:T(8,128)(2,1)}, u32[]{:S(2)}) copy-start(bf16[1,256,384]{2,1,0:T(8,128)(2,1)} %wu_ref.1) | copy-start | bytes 589828
  5.3 0.9 %copy-start.4 = (bf16[1,384,256]{2,1,0:T(8,128)(2,1)S(1)}, bf16[1,384,256]{2,1,0:T(8,128)(2,1)}, u32[]{:S(2)}) copy-start(bf16[1,384,256]{2,1,0:T(8,128)(2,1)} %wd_ref.1) | copy-start | bytes 589828

commit v2 on v0

--- a/solution.py
+++ b/solution.py
@@ -1,6 +1,10 @@
+import functools
+
 import jax
 import jax.numpy as jnp
 from jax import lax
+from jax.experimental import pallas as pl
+from jax.experimental.pallas import tpu as pltpu
 from jax.sharding import PartitionSpec as P
 
 
@@ -28,7 +32,7 @@
     return total + kept.astype(jnp.float32)
 
 
-def per_device(x_rows, expert_ids, gates, cotangent, w_gate, w_up, w_down):
+def collective_device(x_rows, expert_ids, gates, cotangent, w_gate, w_up, w_down):
     full_gate, full_up, full_down = (
         lax.all_gather(w_gate, "dp", axis=1, tiled=True),
         lax.all_gather(w_up, "dp", axis=1, tiled=True),
@@ -138,6 +142,343 @@
     )
 
 
+F32 = jnp.float32
+BF16 = jnp.bfloat16
+
+
+def dot(a, b):
+    return lax.dot_general(a, b, (((1,), (0,)), ((), ())), preferred_element_type=F32)
+
+
+def dot_left_t(a, b):
+    return lax.dot_general(a, b, (((0,), (0,)), ((), ())), preferred_element_type=F32)
+
+
+def dot_right_t(a, b):
+    return lax.dot_general(a, b, (((1,), (1,)), ((), ())), preferred_element_type=F32)
+
+
+def flipped(index, bits, size):
+    result, place = 0, 1
+    while place < size:
+        digit = (index // place) % 2
+        result = result + ((digit + 1) % 2 if bits & place else digit) * place
+        place *= 2
+    return result
+
+
+def layer_kernel(
+    n_dp, n_ex, cap,
+    x_hbm, ids_hbm, gates_hbm, cot_hbm, wg_hbm, wu_hbm, wd_hbm,
+    gated_hbm, igrad_hbm, ggrad_hbm, ogg_hbm, ogu_hbm, ogd_hbm,
+    gated_ref, igrad_ref, ggrad_ref, ogg_ref, ogu_ref, ogd_ref,
+    x_ref, ids_ref, gates_ref, cot_ref,
+    place_ref, send_x, send_s, recv_x, recv_s, out_send, in_send, out_back, in_back,
+    full_g, full_u, full_d, hid_ref, fac_g, fac_u, dg_ref, du_ref,
+    part_g, part_u, part_d, got_g, got_u, got_d, sum_g, sum_u, sum_d,
+    own_sem, out_sem, z_send, z_recv, w_send, w_recv, g_send, g_recv,
+):
+    me_e, me_d = lax.axis_index("expert"), lax.axis_index("dp")
+    z_peers = [(k, flipped(me_e, k, n_ex)) for k in range(n_ex - 1, 0, -1)]
+    side, over, across = (flipped(me_d, k, n_dp) for k in (1, 2, 3))
+    rows, width = x_ref.shape
+    piece = width // n_dp
+
+    barrier = pltpu.get_barrier_semaphore()
+    for _, peer in z_peers:
+        pl.semaphore_signal(barrier, inc=1, device_id={"expert": peer}, device_id_type=pl.DeviceIdType.MESH)
+    for peer in (side, over):
+        pl.semaphore_signal(barrier, inc=1, device_id={"dp": peer}, device_id_type=pl.DeviceIdType.MESH)
+
+    own = []
+    for source, target in (
+        (ids_hbm, ids_ref), (x_hbm, x_ref), (gates_hbm, gates_ref), (cot_hbm, cot_ref),
+        (wg_hbm.at[0], full_g.at[me_d]), (wu_hbm.at[0], full_u.at[me_d]), (wd_hbm.at[0], full_d.at[me_d]),
+    ):
+        copy = pltpu.make_async_copy(source, target, own_sem.at[len(own)])
+        copy.start()
+        own.append(copy)
+
+    def columns(q):
+        return slice(q * piece, (q + 1) * piece)
+
+    copies = []
+
+    def remote(source, target, send_sem, recv_sem, axis, peer):
+        copy = pltpu.make_async_remote_copy(
+            src_ref=source,
+            dst_ref=target,
+            send_sem=send_sem,
+            recv_sem=recv_sem,
+            device_id={axis: peer},
+            device_id_type=pl.DeviceIdType.MESH,
+        )
+        copy.start()
+        copies.append(copy)
+        return copy
+
+    def slots(index):
+        return pl.ds(pl.multiple_of(index * cap, cap), cap)
+
+    def z_start(which, source, target, k):
+        peer = flipped(me_e, k, n_ex)
+        return remote(
+            source.at[slots(peer)], target.at[slots(me_e)],
+            z_send.at[which, k], z_recv.at[which, k], "expert", peer,
+        )
+
+    def z_own(source, target):
+        target[slots(me_e), :] = source[slots(me_e), :]
+
+    def w_start(which, source, target):
+        return [
+            remote(
+                source.at[0], target.at[me_d],
+                w_send.at[which, k], w_recv.at[which, k], "dp", peer,
+            )
+            for k, peer in enumerate((side, over))
+        ]
+
+    def w_pass(which, target, direct):
+        half = target.shape[1] // 2
+        first, second = target.at[side, pl.ds(0, half)], target.at[over, pl.ds(half, half)]
+        direct[0].wait_recv()
+        one = remote(first, first, w_send.at[which, 2], w_recv.at[which, 2], "dp", over)
+        direct[1].wait_recv()
+        two = remote(second, second, w_send.at[which, 3], w_recv.at[which, 3], "dp", side)
+        return [one, two]
+
+    def g_start(which, part, got):
+        half = part.shape[1] // 2
+        upper, lower = pl.ds(0, half), pl.ds(half, half)
+        made = {}
+        for slot, source, peer in (
+            (1, part.at[across, upper], side),
+            (3, part.at[across, lower], over),
+            (0, part.at[side, upper], side),
+            (2, part.at[over, lower], over),
+        ):
+            made[slot] = remote(
+                source, got.at[slot], g_send.at[which, slot], g_recv.at[which, slot], "dp", peer
+            )
+        return made
+
+    def g_pass(which, part, got, total, made):
+        half = part.shape[1] // 2
+        for slot, peer, rows_of in ((1, over, pl.ds(0, half)), (3, side, pl.ds(half, half))):
+            made[slot].wait_recv()
+            index, later = slot // 2, 4 + slot // 2
+            total[index] = (part[peer, rows_of].astype(F32) + got[slot].astype(F32)).astype(BF16)
+            made[later] = remote(
+                total.at[index], got.at[later], g_send.at[which, later], g_recv.at[which, later], "dp", peer
+            )
+
+    def g_finish(part, got, made, out):
+        half = part.shape[1] // 2
+        for slot, later, rows_of in ((0, 4, pl.ds(0, half)), (2, 5, pl.ds(half, half))):
+            made[slot].wait_recv()
+            made[later].wait_recv()
+            out[0, rows_of] = (
+                part[me_d, rows_of].astype(F32) + got[slot].astype(F32) + got[later].astype(F32)
+            ).astype(BF16)
+
+    stored = []
+
+    def store(source, target):
+        copy = pltpu.make_async_copy(source, target, out_sem.at[len(stored)])
+        copy.start()
+        stored.append(copy)
+
+    def arrived(made):
+        for copy in made:
+            copy.wait_recv()
+
+    far = [k for k in range(n_ex - 1, 0, -1) if k >= n_ex // 2]
+    near = [k for k in range(n_ex - 1, 0, -1) if k < n_ex // 2]
+
+    own[0].wait()
+    ids = ids_ref[...]
+    onehot = (ids == lax.broadcasted_iota(jnp.int32, (n_ex, rows), 0)).astype(F32)
+    row_a = lax.broadcasted_iota(jnp.int32, (rows, rows), 0)
+    row_b = lax.broadcasted_iota(jnp.int32, (rows, rows), 1)
+    ranks = jnp.sum(dot(onehot.astype(BF16), (row_a < row_b).astype(BF16)) * onehot, 0, keepdims=True)
+    slot = ids * cap + ranks.astype(jnp.int32)
+    place_ref[...] = (slot == lax.broadcasted_iota(jnp.int32, (n_ex * cap, rows), 0)).astype(BF16)
+    own[1].wait()
+    send_x[...] = dot(place_ref[...], x_ref[...]).astype(BF16)
+
+    pl.semaphore_wait(barrier, n_ex + 1)
+
+    x_copies = [z_start(0, send_x, recv_x, k) for k in far]
+    g_direct = w_start(0, wg_hbm, full_g)
+    u_direct = w_start(1, wu_hbm, full_u)
+
+    own[2].wait()
+    own[3].wait()
+    diagonal = row_a == row_b
+    gates = jnp.sum(jnp.where(diagonal, gates_ref[...], 0.0), 1, keepdims=True)
+    scaled = (gates * cot_ref[...].astype(F32)).astype(BF16)
+    send_s[...] = dot(place_ref[...], scaled).astype(BF16)
+    s_copies = []
+    for step, k in enumerate(far):
+        s_copies.append(z_start(1, send_s, recv_s, k))
+        if step < len(near):
+            x_copies.append(z_start(0, send_x, recv_x, near[step]))
+    s_copies += [z_start(1, send_s, recv_s, k) for k in near]
+    z_own(send_x, recv_x)
+    z_own(send_s, recv_s)
+
+    g_passed = w_pass(0, full_g, g_direct)
+    d_direct = w_start(2, wd_hbm, full_d)
+    u_passed = w_pass(1, full_u, u_direct)
+    hidden_units = wg_hbm.shape[2]
+    arrived(x_copies)
+    arrived(g_passed)
+    own[4].wait()
+    gate_act = dot(recv_x[...], full_g[...].reshape(width, hidden_units))
+    d_passed = w_pass(2, full_d, d_direct)
+    arrived(u_passed)
+    own[5].wait()
+    up_act = dot(recv_x[...], full_u[...].reshape(width, hidden_units))
+    sigma = jax.nn.sigmoid(gate_act)
+    hid_ref[...] = (gate_act * sigma * up_act).astype(BF16)
+    fac_g[...] = up_act * sigma * (1.0 + gate_act * (1.0 - sigma))
+    fac_u[...] = gate_act * sigma
+    arrived(d_passed)
+    own[6].wait()
+    for q in range(n_dp):
+        out_send[:, columns(q)] = dot(hid_ref[...], full_d[q]).astype(BF16)
+    out_copies = [z_start(2, out_send, out_back, k) for k in far + near]
+    z_own(out_send, out_back)
+
+    arrived(s_copies)
+    for q in range(n_dp):
+        part_d[q] = dot_left_t(hid_ref[...], recv_s[:, columns(q)]).astype(BF16)
+    pd_copies = g_start(2, part_d, got_d)
+    backed = dot_right_t(recv_s[:, columns(0)], full_d[0])
+    for q in range(1, n_dp):
+        backed = backed + dot_right_t(recv_s[:, columns(q)], full_d[q])
+    dg_ref[...] = (backed * fac_g[...]).astype(BF16)
+    du_ref[...] = (backed * fac_u[...]).astype(BF16)
+    for q in range(n_dp):
+        part_g[q] = dot_left_t(recv_x[:, columns(q)], dg_ref[...]).astype(BF16)
+    pg_copies = g_start(0, part_g, got_g)
+    for q in range(n_dp):
+        part_u[q] = dot_left_t(recv_x[:, columns(q)], du_ref[...]).astype(BF16)
+    pu_copies = g_start(1, part_u, got_u)
+    for q in range(n_dp):
+        in_send[:, columns(q)] = (
+            dot_right_t(dg_ref[...], full_g[q]) + dot_right_t(du_ref[...], full_u[q])
+        ).astype(BF16)
+    in_copies = [z_start(3, in_send, in_back, k) for k in far + near]
+    z_own(in_send, in_back)
+    g_pass(2, part_d, got_d, sum_d, pd_copies)
+    g_pass(0, part_g, got_g, sum_g, pg_copies)
+    g_pass(1, part_u, got_u, sum_u, pu_copies)
+
+    arrived(out_copies)
+    row_out = dot_left_t(place_ref[...], out_back[...])
+    gated_ref[...] = (gates * row_out).astype(BF16)
+    row_sums = jnp.sum(cot_ref[...].astype(F32) * row_out, 1, keepdims=True)
+    ggrad_ref[...] = jnp.sum(jnp.where(diagonal, row_sums, 0.0), 0, keepdims=True)
+    store(gated_ref, gated_hbm)
+    store(ggrad_ref, ggrad_hbm)
+    g_finish(part_d, got_d, pd_copies, ogd_ref)
+    store(ogd_ref, ogd_hbm)
+    g_finish(part_g, got_g, pg_copies, ogg_ref)
+    store(ogg_ref, ogg_hbm)
+    g_finish(part_u, got_u, pu_copies, ogu_ref)
+    store(ogu_ref, ogu_hbm)
+    arrived(in_copies)
+    igrad_ref[...] = dot_left_t(place_ref[...], in_back[...]).astype(BF16)
+    store(igrad_ref, igrad_hbm)
+    for copy in copies:
+        copy.wait_send()
+    for copy in stored:
+        copy.wait()
+
+
+def results_kernel(*refs):
+    count = len(refs) // 2
+    sources, targets, sem = refs[:count], refs[count:-1], refs[-1]
+    made = [
+        pltpu.make_async_copy(source, target, sem.at[i])
+        for i, (source, target) in enumerate(zip(sources, targets))
+    ]
+    for copy in made:
+        copy.start()
+    for copy in made:
+        copy.wait()
+
+
+def power_of_two(size):
+    return size & (size - 1) == 0
+
+
+def per_device(x_rows, expert_ids, gates, cotangent, w_gate, w_up, w_down):
+    n_dp, n_ex = lax.axis_size("dp"), lax.axis_size("expert")
+    rows, width = x_rows.shape
+    cap = 2 * rows // n_ex
+    _, piece, hidden = w_gate.shape
+    if cap % 16 or piece % 32 or hidden % 32 or not power_of_two(n_ex) or n_dp != 4:
+        return collective_device(x_rows, expert_ids, gates, cotangent, w_gate, w_up, w_down)
+    total = n_ex * cap
+    hbm = pl.BlockSpec(memory_space=pltpu.HBM)
+    slots_of = pltpu.VMEM((total, width), BF16)
+    gates_of = pltpu.VMEM((n_dp, piece, hidden), BF16)
+    downs_of = pltpu.VMEM((n_dp, hidden, piece), BF16)
+    got_gates = pltpu.VMEM((6, piece // 2, hidden), BF16)
+    got_downs = pltpu.VMEM((6, hidden // 2, piece), BF16)
+    sum_gates = pltpu.VMEM((2, piece // 2, hidden), BF16)
+    sum_downs = pltpu.VMEM((2, hidden // 2, piece), BF16)
+    acts_of = pltpu.VMEM((total, hidden), BF16)
+    facs_of = pltpu.VMEM((total, hidden), F32)
+    shapes = (
+        jax.ShapeDtypeStruct((rows, width), BF16),
+        jax.ShapeDtypeStruct((rows, width), BF16),
+        jax.ShapeDtypeStruct((1, rows), F32),
+        jax.ShapeDtypeStruct(w_gate.shape, BF16),
+        jax.ShapeDtypeStruct(w_up.shape, BF16),
+        jax.ShapeDtypeStruct(w_down.shape, BF16),
+    )
+    results = pl.pallas_call(
+        functools.partial(layer_kernel, n_dp, n_ex, cap),
+        out_shape=shapes,
+        in_specs=[hbm] * 7,
+        out_specs=[hbm] * 6,
+        scratch_shapes=[
+            *(pltpu.VMEM(shape.shape, shape.dtype) for shape in shapes),
+            pltpu.VMEM((rows, width), BF16), pltpu.VMEM((1, rows), jnp.int32),
+            pltpu.VMEM((1, rows), F32), pltpu.VMEM((rows, width), BF16),
+            pltpu.VMEM((total, rows), BF16),
+            slots_of, slots_of, slots_of, slots_of, slots_of, slots_of, slots_of, slots_of,
+            gates_of, gates_of, downs_of,
+            acts_of, facs_of, facs_of, acts_of, acts_of,
+            gates_of, gates_of, downs_of,
+            got_gates, got_gates, got_downs, sum_gates, sum_gates, sum_downs,
+            pltpu.SemaphoreType.DMA((7,)), pltpu.SemaphoreType.DMA((6,)),
+            pltpu.SemaphoreType.DMA((4, n_ex)), pltpu.SemaphoreType.DMA((4, n_ex)),
+            pltpu.SemaphoreType.DMA((3, 4)), pltpu.SemaphoreType.DMA((3, 4)),
+            pltpu.SemaphoreType.DMA((3, 6)), pltpu.SemaphoreType.DMA((3, 6)),
+        ],
+        compiler_params=pltpu.CompilerParams(
+            collective_id=0, has_side_effects=True, vmem_limit_bytes=64 * 1024 * 1024
+        ),
+    )(
+        x_rows, expert_ids.reshape(1, rows), gates.reshape(1, rows), cotangent,
+        w_gate, w_up, w_down,
+    )
+    results = pl.pallas_call(
+        results_kernel,
+        out_shape=shapes,
+        in_specs=[hbm] * 6,
+        out_specs=[hbm] * 6,
+        scratch_shapes=[pltpu.SemaphoreType.DMA((6,))],
+        compiler_params=pltpu.CompilerParams(vmem_limit_bytes=64 * 1024 * 1024),
+    )(*results)
+    return (*results[:2], results[2].reshape(rows, 1), *results[3:])
+
+
 def solution(mesh):
     in_specs = (
         P(("dp", "expert"), None),

time: 167 us -> 89.5 us (0.54)
  Pallas kernels: 0 us -> 88.7 us
  blocking collectives: 77.3 us -> 0 us
  starting transfers between devices: 25.9 us -> 0 us
  matrix products: 24.3 us -> 0 us
  waiting for transfers between devices: 21.1 us -> 0 us
  local copies, waits for them, and re-layouts: 9.76 us -> 0 us
  other arithmetic: 6.15 us -> 0 us
    pallas_call x0 -> x2, Pallas kernels: none -> 88.7 us  [the longest x1 53.8 us: per_device(): pl.pallas_call(functools.partial(layer_kernel, n_dp, n_ex, cap), out_shap...]
    all_gather x6 -> x0, blocking collectives: 77.3 us -> none  [the longest x1 15.3 us: per_device(): lax.all_gather(w_down, 'dp', axis=2, tiled=True)]
    all_to_all x6 -> x0, starting transfers between devices: 25.9 us -> none  [the longest x1 6.46 us: per_device(): lax.all_to_all(send_in, 'expert', split_axis=0, concat_axis=0, tiled=True)]
    dot_general x18 -> x0, matrix products: 24.3 us -> none  [the longest x4 7.4 us: per_device(): jnp.dot(group_in.T, group_dup, preferred_element_type=jnp.float32)]
    all_to_all x6 -> x0, waiting for transfers between devices: 21.1 us -> none  [the longest x1 11.5 us: per_device(): lax.all_to_all(slot_out.reshape(experts, capacity, width), 'expert', spli...]
    all_to_all x4 -> x0, local copies, waits for them, and re-layouts: 2.48 us -> none  [the longest x2 1.25 us: per_device(): lax.all_to_all(flat_scaled, 'dp', split_axis=1, concat_axis=0, tiled=True)]
    unnamed x46 -> x0, local copies, waits for them, and re-layouts: 2.46 us -> none
    convert_element_type x4 -> x0, other arithmetic: 2.43 us -> none  [the longest x1 0.79 us: per_device(): summed_down.astype(jnp.bfloat16)]
  transfers between devices with their start and end apart: 6 -> 0, of which waited for: 2 -> 0; matrix products, arithmetic and copies ran while one was open for 17% -> 0% of each run, Pallas kernels for 0% -> 0%
where the time goes in v2:
time: 89.5 us; the launch traced here: 89.4 us
  Pallas kernels  88.7 us (99%)
    pallas_call x1, Pallas kernels, per_device(): pl.pallas_call(functools.partial(layer_kernel, n_dp, n_ex, cap), out_shap...  53.8 us
    pallas_call x1, Pallas kernels, per_device(): pl.pallas_call(results_kernel, out_shape=shapes, in_specs=[hbm] * 6, out_...  34.9 us

profile of v2, /device:TPU:0, one launch (start us, length us, event | category | flops | bytes accessed | tf_op | source)
XLA Modules:
  0.0 89.4 jit_solution(5320308355805388289)
XLA Ops:
  0.6 53.8 %shard_map.118 = (bf16[128,1024]{1,0:T(8,128)(2,1)}, bf16[128,1024]{1,0:T(8,128)(2,1)}, f32[1,128]{1,0:T(1,128)}, bf16[1,256,384]{2,1,0:T(8,128)(2,1)}, bf16[1,2...) custom-call(bf16[128,1024]{1,0:T(8,128)(2,1)} %x_hbm.1, s32[1,128]{1,0:T(1,128)} %bitcast.3, f32[1,128]{1,0:T(1,128)} %bitcast.4, ...), custom_call_target="tpu_custom_call" | custom-call | tf_op jit(solution)/shard_map/pallas_call | solution.py:444
  54.4 34.9 %shard_map.119 = (bf16[128,1024]{1,0:T(8,128)(2,1)}, bf16[128,1024]{1,0:T(8,128)(2,1)}, f32[1,128]{1,0:T(1,128)}, bf16[1,256,384]{2,1,0:T(8,128)(2,1)}, bf16[1,2...) custom-call(bf16[128,1024]{1,0:T(8,128)(2,1)} %get-tuple-element.18.refs_0_, ...), custom_call_target="tpu_custom_call" | custom-call | tf_op jit(solution)/shard_map/pallas_call | solution.py:471

commit v3 on v2

--- a/solution.py
+++ b/solution.py
@@ -399,16 +399,18 @@
 
 
 def results_kernel(*refs):
-    count = len(refs) // 2
-    sources, targets, sem = refs[:count], refs[count:-1], refs[-1]
-    made = [
-        pltpu.make_async_copy(source, target, sem.at[i])
-        for i, (source, target) in enumerate(zip(sources, targets))
-    ]
-    for copy in made:
-        copy.start()
-    for copy in made:
-        copy.wait()
+    count = len(refs) // 3
+    sources, targets, held = refs[:count], refs[count : 2 * count], refs[2 * count : 3 * count]
+    in_sem, out_sem = refs[3 * count :]
+    reads = [pltpu.make_async_copy(sources[i], held[i], in_sem.at[i]) for i in range(count)]
+    writes = [pltpu.make_async_copy(held[i], targets[i], out_sem.at[i]) for i in range(count)]
+    for read in reads:
+        read.start()
+    for read, write in zip(reads, writes):
+        read.wait()
+        write.start()
+    for write in writes:
+        write.wait()
 
 
 def power_of_two(size):
@@ -473,7 +475,10 @@
         out_shape=shapes,
         in_specs=[hbm] * 6,
         out_specs=[hbm] * 6,
-        scratch_shapes=[pltpu.SemaphoreType.DMA((6,))],
+        scratch_shapes=[
+            *(pltpu.VMEM(shape.shape, shape.dtype) for shape in shapes),
+            pltpu.SemaphoreType.DMA((6,)), pltpu.SemaphoreType.DMA((6,)),
+        ],
         compiler_params=pltpu.CompilerParams(vmem_limit_bytes=64 * 1024 * 1024),
     )(*results)
     return (*results[:2], results[2].reshape(rows, 1), *results[3:])

time: 89.5 us -> 56.6 us (0.63)
  Pallas kernels: 88.7 us -> 55.8 us
    pallas_call x1, Pallas kernels: 34.9 us -> 2.04 us  [per_device(): pl.pallas_call(results_kernel, out_shape=shapes, in_specs=[hbm] * 6, out_...]
where the time goes in v3:
time: 56.6 us; the launch traced here: 56.5 us
  Pallas kernels  55.8 us (99%)
  between operations  0.64 us (1%)
    pallas_call x1, Pallas kernels, per_device(): pl.pallas_call(functools.partial(layer_kernel, n_dp, n_ex, cap), out_shap...  53.8 us
    pallas_call x1, Pallas kernels, per_device(): pl.pallas_call(results_kernel, out_shape=shapes, in_specs=[hbm] * 6, out_...  2.04 us

profile of v3, /device:TPU:0, one launch (start us, length us, event | category | flops | bytes accessed | tf_op | source)
XLA Modules:
  0.0 56.5 jit_solution(16055975200797026535)
XLA Ops:
  0.6 53.8 %shard_map.118 = (bf16[128,1024]{1,0:T(8,128)(2,1)}, bf16[128,1024]{1,0:T(8,128)(2,1)}, f32[1,128]{1,0:T(1,128)}, bf16[1,256,384]{2,1,0:T(8,128)(2,1)}, bf16[1,2...) custom-call(bf16[128,1024]{1,0:T(8,128)(2,1)} %x_hbm.1, s32[1,128]{1,0:T(1,128)} %bitcast.3, f32[1,128]{1,0:T(1,128)} %bitcast.4, ...), custom_call_target="tpu_custom_call" | custom-call | tf_op jit(solution)/shard_map/pallas_call | solution.py:446
  54.4 2.0 %shard_map.119 = (bf16[128,1024]{1,0:T(8,128)(2,1)}, bf16[128,1024]{1,0:T(8,128)(2,1)}, f32[1,128]{1,0:T(1,128)}, bf16[1,256,384]{2,1,0:T(8,128)(2,1)}, bf16[1,2...) custom-call(bf16[128,1024]{1,0:T(8,128)(2,1)} %get-tuple-element.18.refs_0_, ...), custom_call_target="tpu_custom_call" | custom-call | tf_op jit(solution)/shard_map/pallas_call | solution.py:473

commit v4 on v3

--- a/solution.py
+++ b/solution.py
@@ -170,11 +170,11 @@
 def layer_kernel(
     n_dp, n_ex, cap,
     x_hbm, ids_hbm, gates_hbm, cot_hbm, wg_hbm, wu_hbm, wd_hbm,
-    gated_hbm, igrad_hbm, ggrad_hbm, ogg_hbm, ogu_hbm, ogd_hbm,
-    gated_ref, igrad_ref, ggrad_ref, ogg_ref, ogu_ref, ogd_ref,
+    gated_hbm, in_back, ggrad_hbm, ogg_hbm, ogu_hbm, ogd_hbm, place_hbm,
+    gated_ref, ggrad_ref, ogg_ref, ogu_ref, ogd_ref, row_place,
     x_ref, ids_ref, gates_ref, cot_ref,
-    place_ref, send_x, send_s, recv_x, recv_s, out_send, in_send, out_back, in_back,
-    full_g, full_u, full_d, hid_ref, fac_g, fac_u, dg_ref, du_ref,
+    place_ref, send_x, send_s, recv_x, recv_s, out_send, in_send, out_back,
+    full_g, full_u, full_d, hid_ref, fac_g, fac_u, dg_ref, du_ref, x_turned, hid_turned,
     part_g, part_u, part_d, got_g, got_u, got_d, sum_g, sum_u, sum_d,
     own_sem, out_sem, z_send, z_recv, w_send, w_recv, g_send, g_recv,
 ):
@@ -304,6 +304,9 @@
     ranks = jnp.sum(dot(onehot.astype(BF16), (row_a < row_b).astype(BF16)) * onehot, 0, keepdims=True)
     slot = ids * cap + ranks.astype(jnp.int32)
     place_ref[...] = (slot == lax.broadcasted_iota(jnp.int32, (n_ex * cap, rows), 0)).astype(BF16)
+    diagonal = row_a == row_b
+    slot_of_row = jnp.sum(jnp.where(diagonal, slot, 0), 1, keepdims=True)
+    row_place[...] = (slot_of_row == lax.broadcasted_iota(jnp.int32, (rows, n_ex * cap), 1)).astype(BF16)
     own[1].wait()
     send_x[...] = dot(place_ref[...], x_ref[...]).astype(BF16)
 
@@ -315,7 +318,6 @@
 
     own[2].wait()
     own[3].wait()
-    diagonal = row_a == row_b
     gates = jnp.sum(jnp.where(diagonal, gates_ref[...], 0.0), 1, keepdims=True)
     scaled = (gates * cot_ref[...].astype(F32)).astype(BF16)
     send_s[...] = dot(place_ref[...], scaled).astype(BF16)
@@ -327,6 +329,7 @@
     s_copies += [z_start(1, send_s, recv_s, k) for k in near]
     z_own(send_x, recv_x)
     z_own(send_s, recv_s)
+    store(row_place, place_hbm)
 
     g_passed = w_pass(0, full_g, g_direct)
     d_direct = w_start(2, wd_hbm, full_d)
@@ -350,10 +353,12 @@
         out_send[:, columns(q)] = dot(hid_ref[...], full_d[q]).astype(BF16)
     out_copies = [z_start(2, out_send, out_back, k) for k in far + near]
     z_own(out_send, out_back)
+    x_turned[...] = recv_x[...].T
+    hid_turned[...] = hid_ref[...].T
 
     arrived(s_copies)
     for q in range(n_dp):
-        part_d[q] = dot_left_t(hid_ref[...], recv_s[:, columns(q)]).astype(BF16)
+        part_d[q] = dot(hid_turned[...], recv_s[:, columns(q)]).astype(BF16)
     pd_copies = g_start(2, part_d, got_d)
     backed = dot_right_t(recv_s[:, columns(0)], full_d[0])
     for q in range(1, n_dp):
@@ -361,23 +366,23 @@
     dg_ref[...] = (backed * fac_g[...]).astype(BF16)
     du_ref[...] = (backed * fac_u[...]).astype(BF16)
     for q in range(n_dp):
-        part_g[q] = dot_left_t(recv_x[:, columns(q)], dg_ref[...]).astype(BF16)
+        part_g[q] = dot(x_turned[columns(q), :], dg_ref[...]).astype(BF16)
     pg_copies = g_start(0, part_g, got_g)
     for q in range(n_dp):
-        part_u[q] = dot_left_t(recv_x[:, columns(q)], du_ref[...]).astype(BF16)
+        part_u[q] = dot(x_turned[columns(q), :], du_ref[...]).astype(BF16)
     pu_copies = g_start(1, part_u, got_u)
     for q in range(n_dp):
         in_send[:, columns(q)] = (
             dot_right_t(dg_ref[...], full_g[q]) + dot_right_t(du_ref[...], full_u[q])
         ).astype(BF16)
     in_copies = [z_start(3, in_send, in_back, k) for k in far + near]
-    z_own(in_send, in_back)
+    store(in_send.at[slots(me_e)], in_back.at[slots(me_e)])
     g_pass(2, part_d, got_d, sum_d, pd_copies)
     g_pass(0, part_g, got_g, sum_g, pg_copies)
     g_pass(1, part_u, got_u, sum_u, pu_copies)
 
     arrived(out_copies)
-    row_out = dot_left_t(place_ref[...], out_back[...])
+    row_out = dot(row_place[...], out_back[...])
     gated_ref[...] = (gates * row_out).astype(BF16)
     row_sums = jnp.sum(cot_ref[...].astype(F32) * row_out, 1, keepdims=True)
     ggrad_ref[...] = jnp.sum(jnp.where(diagonal, row_sums, 0.0), 0, keepdims=True)
@@ -390,8 +395,6 @@
     g_finish(part_u, got_u, pu_copies, ogu_ref)
     store(ogu_ref, ogu_hbm)
     arrived(in_copies)
-    igrad_ref[...] = dot_left_t(place_ref[...], in_back[...]).astype(BF16)
-    store(igrad_ref, igrad_hbm)
     for copy in copies:
         copy.wait_send()
     for copy in stored:
@@ -399,17 +402,27 @@
 
 
 def results_kernel(*refs):
-    count = len(refs) // 3
-    sources, targets, held = refs[:count], refs[count : 2 * count], refs[2 * count : 3 * count]
-    in_sem, out_sem = refs[3 * count :]
-    reads = [pltpu.make_async_copy(sources[i], held[i], in_sem.at[i]) for i in range(count)]
-    writes = [pltpu.make_async_copy(held[i], targets[i], out_sem.at[i]) for i in range(count)]
-    for read in reads:
+    back_hbm, place_hbm, *sources = refs[:7]
+    igrad_hbm, *targets = refs[7:13]
+    back, place, igrad, *held = refs[13:21]
+    in_sem, out_sem = refs[21:]
+    first = [
+        pltpu.make_async_copy(back_hbm, back, in_sem.at[5]),
+        pltpu.make_async_copy(place_hbm, place, in_sem.at[6]),
+    ]
+    reads = [pltpu.make_async_copy(sources[i], held[i], in_sem.at[i]) for i in range(5)]
+    writes = [pltpu.make_async_copy(held[i], targets[i], out_sem.at[i]) for i in range(5)]
+    for read in first + reads:
         read.start()
+    for read in first:
+        read.wait()
+    igrad[...] = dot(place[...], back[...]).astype(BF16)
+    last = pltpu.make_async_copy(igrad, igrad_hbm, out_sem.at[5])
+    last.start()
     for read, write in zip(reads, writes):
         read.wait()
         write.start()
-    for write in writes:
+    for write in writes + [last]:
         write.wait()
 
 
@@ -437,28 +450,30 @@
     facs_of = pltpu.VMEM((total, hidden), F32)
     shapes = (
         jax.ShapeDtypeStruct((rows, width), BF16),
-        jax.ShapeDtypeStruct((rows, width), BF16),
         jax.ShapeDtypeStruct((1, rows), F32),
         jax.ShapeDtypeStruct(w_gate.shape, BF16),
         jax.ShapeDtypeStruct(w_up.shape, BF16),
         jax.ShapeDtypeStruct(w_down.shape, BF16),
     )
-    results = pl.pallas_call(
+    back_shape = jax.ShapeDtypeStruct((total, width), BF16)
+    place_shape = jax.ShapeDtypeStruct((rows, total), BF16)
+    gated, back, *others, place = pl.pallas_call(
         functools.partial(layer_kernel, n_dp, n_ex, cap),
-        out_shape=shapes,
+        out_shape=(shapes[0], back_shape, *shapes[1:], place_shape),
         in_specs=[hbm] * 7,
-        out_specs=[hbm] * 6,
+        out_specs=[hbm] * 7,
         scratch_shapes=[
-            *(pltpu.VMEM(shape.shape, shape.dtype) for shape in shapes),
+            *(pltpu.VMEM(shape.shape, shape.dtype) for shape in (*shapes, place_shape)),
             pltpu.VMEM((rows, width), BF16), pltpu.VMEM((1, rows), jnp.int32),
             pltpu.VMEM((1, rows), F32), pltpu.VMEM((rows, width), BF16),
             pltpu.VMEM((total, rows), BF16),
-            slots_of, slots_of, slots_of, slots_of, slots_of, slots_of, slots_of, slots_of,
+            slots_of, slots_of, slots_of, slots_of, slots_of, slots_of, slots_of,
             gates_of, gates_of, downs_of,
             acts_of, facs_of, facs_of, acts_of, acts_of,
+            pltpu.VMEM((width, total), BF16), pltpu.VMEM((hidden, total), BF16),
             gates_of, gates_of, downs_of,
             got_gates, got_gates, got_downs, sum_gates, sum_gates, sum_downs,
-            pltpu.SemaphoreType.DMA((7,)), pltpu.SemaphoreType.DMA((6,)),
+            pltpu.SemaphoreType.DMA((7,)), pltpu.SemaphoreType.DMA((7,)),
             pltpu.SemaphoreType.DMA((4, n_ex)), pltpu.SemaphoreType.DMA((4, n_ex)),
             pltpu.SemaphoreType.DMA((3, 4)), pltpu.SemaphoreType.DMA((3, 4)),
             pltpu.SemaphoreType.DMA((3, 6)), pltpu.SemaphoreType.DMA((3, 6)),
@@ -470,18 +485,19 @@
         x_rows, expert_ids.reshape(1, rows), gates.reshape(1, rows), cotangent,
         w_gate, w_up, w_down,
     )
-    results = pl.pallas_call(
+    igrad_shape = jax.ShapeDtypeStruct((rows, width), BF16)
+    input_grad, gated_out, gate_grad, *weight_grads = pl.pallas_call(
         results_kernel,
-        out_shape=shapes,
-        in_specs=[hbm] * 6,
+        out_shape=(igrad_shape, *shapes),
+        in_specs=[hbm] * 7,
         out_specs=[hbm] * 6,
         scratch_shapes=[
-            *(pltpu.VMEM(shape.shape, shape.dtype) for shape in shapes),
-            pltpu.SemaphoreType.DMA((6,)), pltpu.SemaphoreType.DMA((6,)),
+            *(pltpu.VMEM(shape.shape, shape.dtype) for shape in (back_shape, place_shape, igrad_shape, *shapes)),
+            pltpu.SemaphoreType.DMA((7,)), pltpu.SemaphoreType.DMA((6,)),
         ],
         compiler_params=pltpu.CompilerParams(vmem_limit_bytes=64 * 1024 * 1024),
-    )(*results)
-    return (*results[:2], results[2].reshape(rows, 1), *results[3:])
+    )(back, place, gated, *others)
+    return (gated_out, input_grad, gate_grad.reshape(rows, 1), *weight_grads)
 
 
 def solution(mesh):

time: 56.6 us -> 56.2 us (level)
    pallas_call x1, Pallas kernels: 53.8 us -> 53.1 us  [per_device(): pl.pallas_call(functools.partial(layer_kernel, n_dp, n_ex, cap), out_shap...]
where the time goes in v4:
time: 56.2 us; the launch traced here: 56.1 us
  Pallas kernels  55.4 us (99%)
  between operations  0.64 us (1%)
    pallas_call x1, Pallas kernels, per_device(): pl.pallas_call(functools.partial(layer_kernel, n_dp, n_ex, cap), out_shap...  53.1 us
    pallas_call x1, Pallas kernels, per_device(): pl.pallas_call(results_kernel, out_shape=(igrad_shape, *shapes), in_specs...  2.38 us

profile of v4, /device:TPU:0, one launch (start us, length us, event | category | flops | bytes accessed | tf_op | source)
XLA Modules:
  0.0 56.1 jit_solution(6995293701671801445)
XLA Ops:
  0.6 53.1 %shard_map.118 = (bf16[128,1024]{1,0:T(8,128)(2,1)}, bf16[256,1024]{1,0:T(8,128)(2,1)}, f32[1,128]{1,0:T(1,128)}, bf16[1,256,384]{2,1,0:T(8,128)(2,1)}, bf16[1,2...) custom-call(bf16[128,1024]{1,0:T(8,128)(2,1)} %x_hbm.1, s32[1,128]{1,0:T(1,128)} %bitcast.3, ...), custom_call_target="tpu_custom_call" | custom-call | tf_op jit(solution)/shard_map/pallas_call | solution.py:460
  53.7 2.4 %shard_map.119 = (bf16[128,1024]{1,0:T(8,128)(2,1)}, bf16[128,1024]{1,0:T(8,128)(2,1)}, f32[1,128]{1,0:T(1,128)}, bf16[1,256,384]{2,1,0:T(8,128)(2,1)}, bf16[1,2...) custom-call(bf16[256,1024]{1,0:T(8,128)(2,1)} %get-tuple-element.19.refs_0_, ...), custom_call_target="tpu_custom_call" | custom-call | tf_op jit(solution)/shard_map/pallas_call | solution.py:489

commit v5 on v4

--- a/solution.py
+++ b/solution.py
@@ -161,8 +161,7 @@
 def flipped(index, bits, size):
     result, place = 0, 1
     while place < size:
-        digit = (index // place) % 2
-        result = result + ((digit + 1) % 2 if bits & place else digit) * place
+        result = result + ((index // place) % 2 + (bits // place) % 2) % 2 * place
         place *= 2
     return result
 
@@ -220,12 +219,30 @@
     def slots(index):
         return pl.ds(pl.multiple_of(index * cap, cap), cap)
 
-    def z_start(which, source, target, k):
+    quarter = n_ex // 4
+    outer = 1 - (me_e // quarter + 1) // 2 % 2
+
+    def z_partner(turn):
+        last = n_ex - 2 - turn
+        return (last + (n_ex // 2 - 1) * outer) % (n_ex - 1) + 1
+
+    def z_copy(which, source, target, k):
         peer = flipped(me_e, k, n_ex)
-        return remote(
-            source.at[slots(peer)], target.at[slots(me_e)],
-            z_send.at[which, k], z_recv.at[which, k], "expert", peer,
+        return pltpu.make_async_remote_copy(
+            src_ref=source.at[slots(peer)],
+            dst_ref=target.at[slots(me_e)],
+            send_sem=z_send.at[which, k],
+            recv_sem=z_recv.at[which, k],
+            device_id={"expert": peer},
+            device_id_type=pl.DeviceIdType.MESH,
         )
+
+    def z_start(which, source, target):
+        for turn in range(n_ex - 1):
+            z_copy(which, source, target, z_partner(turn)).start()
+        made = [z_copy(which, source, target, k) for k in range(1, n_ex)]
+        copies.extend(made)
+        return made
 
     def z_own(source, target):
         target[slots(me_e), :] = source[slots(me_e), :]
@@ -293,9 +310,6 @@
         for copy in made:
             copy.wait_recv()
 
-    far = [k for k in range(n_ex - 1, 0, -1) if k >= n_ex // 2]
-    near = [k for k in range(n_ex - 1, 0, -1) if k < n_ex // 2]
-
     own[0].wait()
     ids = ids_ref[...]
     onehot = (ids == lax.broadcasted_iota(jnp.int32, (n_ex, rows), 0)).astype(F32)
@@ -312,7 +326,7 @@
 
     pl.semaphore_wait(barrier, n_ex + 1)
 
-    x_copies = [z_start(0, send_x, recv_x, k) for k in far]
+    x_copies = z_start(0, send_x, recv_x)
     g_direct = w_start(0, wg_hbm, full_g)
     u_direct = w_start(1, wu_hbm, full_u)
 
@@ -321,12 +335,7 @@
     gates = jnp.sum(jnp.where(diagonal, gates_ref[...], 0.0), 1, keepdims=True)
     scaled = (gates * cot_ref[...].astype(F32)).astype(BF16)
     send_s[...] = dot(place_ref[...], scaled).astype(BF16)
-    s_copies = []
-    for step, k in enumerate(far):
-        s_copies.append(z_start(1, send_s, recv_s, k))
-        if step < len(near):
-            x_copies.append(z_start(0, send_x, recv_x, near[step]))
-    s_copies += [z_start(1, send_s, recv_s, k) for k in near]
+    s_copies = z_start(1, send_s, recv_s)
     z_own(send_x, recv_x)
     z_own(send_s, recv_s)
     store(row_place, place_hbm)
@@ -351,7 +360,7 @@
     own[6].wait()
     for q in range(n_dp):
         out_send[:, columns(q)] = dot(hid_ref[...], full_d[q]).astype(BF16)
-    out_copies = [z_start(2, out_send, out_back, k) for k in far + near]
+    out_copies = z_start(2, out_send, out_back)
     z_own(out_send, out_back)
     x_turned[...] = recv_x[...].T
     hid_turned[...] = hid_ref[...].T
@@ -375,7 +384,7 @@
         in_send[:, columns(q)] = (
             dot_right_t(dg_ref[...], full_g[q]) + dot_right_t(du_ref[...], full_u[q])
         ).astype(BF16)
-    in_copies = [z_start(3, in_send, in_back, k) for k in far + near]
+    in_copies = z_start(3, in_send, in_back)
     store(in_send.at[slots(me_e)], in_back.at[slots(me_e)])
     g_pass(2, part_d, got_d, sum_d, pd_copies)
     g_pass(0, part_g, got_g, sum_g, pg_copies)
@@ -435,7 +444,7 @@
     rows, width = x_rows.shape
     cap = 2 * rows // n_ex
     _, piece, hidden = w_gate.shape
-    if cap % 16 or piece % 32 or hidden % 32 or not power_of_two(n_ex) or n_dp != 4:
+    if cap % 16 or piece % 32 or hidden % 32 or not power_of_two(n_ex) or n_ex < 4 or n_dp != 4:
         return collective_device(x_rows, expert_ids, gates, cotangent, w_gate, w_up, w_down)
     total = n_ex * cap
     hbm = pl.BlockSpec(memory_space=pltpu.HBM)

time: 56.2 us -> 56.3 us (level)
  no operation moved by 1% of the time
where the time goes in v5:
time: 56.3 us; the launch traced here: 56.1 us
  Pallas kernels  55.4 us (98%)
  between operations  0.64 us (1%)
    pallas_call x1, Pallas kernels, per_device(): pl.pallas_call(functools.partial(layer_kernel, n_dp, n_ex, cap), out_shap...  53.1 us
    pallas_call x1, Pallas kernels, per_device(): pl.pallas_call(results_kernel, out_shape=(igrad_shape, *shapes), in_specs...  2.38 us

profile of v5, /device:TPU:0, one launch (start us, length us, event | category | flops | bytes accessed | tf_op | source)
XLA Modules:
  0.0 56.1 jit_solution(2047670116051324369)
XLA Ops:
  0.6 53.1 %shard_map.118 = (bf16[128,1024]{1,0:T(8,128)(2,1)}, bf16[256,1024]{1,0:T(8,128)(2,1)}, f32[1,128]{1,0:T(1,128)}, bf16[1,256,384]{2,1,0:T(8,128)(2,1)}, bf16[1,2...) custom-call(bf16[128,1024]{1,0:T(8,128)(2,1)} %x_hbm.1, s32[1,128]{1,0:T(1,128)} %bitcast.3, ...), custom_call_target="tpu_custom_call" | custom-call | tf_op jit(solution)/shard_map/pallas_call | solution.py:469
  53.7 2.4 %shard_map.119 = (bf16[128,1024]{1,0:T(8,128)(2,1)}, bf16[128,1024]{1,0:T(8,128)(2,1)}, f32[1,128]{1,0:T(1,128)}, bf16[1,256,384]{2,1,0:T(8,128)(2,1)}, bf16[1,2...) custom-call(bf16[256,1024]{1,0:T(8,128)(2,1)} %get-tuple-element.19.refs_0_, ...), custom_call_target="tpu_custom_call" | custom-call | tf_op jit(solution)/shard_map/pallas_call | solution.py:498

commit v6 on v4

--- a/solution.py
+++ b/solution.py
@@ -304,38 +304,39 @@
     ranks = jnp.sum(dot(onehot.astype(BF16), (row_a < row_b).astype(BF16)) * onehot, 0, keepdims=True)
     slot = ids * cap + ranks.astype(jnp.int32)
     place_ref[...] = (slot == lax.broadcasted_iota(jnp.int32, (n_ex * cap, rows), 0)).astype(BF16)
-    diagonal = row_a == row_b
-    slot_of_row = jnp.sum(jnp.where(diagonal, slot, 0), 1, keepdims=True)
-    row_place[...] = (slot_of_row == lax.broadcasted_iota(jnp.int32, (rows, n_ex * cap), 1)).astype(BF16)
     own[1].wait()
     send_x[...] = dot(place_ref[...], x_ref[...]).astype(BF16)
 
     pl.semaphore_wait(barrier, n_ex + 1)
 
-    x_copies = [z_start(0, send_x, recv_x, k) for k in far]
+    x_far = [z_start(0, send_x, recv_x, k) for k in far]
     g_direct = w_start(0, wg_hbm, full_g)
     u_direct = w_start(1, wu_hbm, full_u)
+    x_near = [z_start(0, send_x, recv_x, k) for k in near]
 
     own[2].wait()
     own[3].wait()
+    diagonal = row_a == row_b
     gates = jnp.sum(jnp.where(diagonal, gates_ref[...], 0.0), 1, keepdims=True)
     scaled = (gates * cot_ref[...].astype(F32)).astype(BF16)
     send_s[...] = dot(place_ref[...], scaled).astype(BF16)
-    s_copies = []
-    for step, k in enumerate(far):
-        s_copies.append(z_start(1, send_s, recv_s, k))
-        if step < len(near):
-            x_copies.append(z_start(0, send_x, recv_x, near[step]))
-    s_copies += [z_start(1, send_s, recv_s, k) for k in near]
+    s_copies = [z_start(1, send_s, recv_s, k) for k in near]
+    slot_of_row = jnp.sum(jnp.where(diagonal, slot, 0), 1, keepdims=True)
+    row_place[...] = (slot_of_row == lax.broadcasted_iota(jnp.int32, (rows, n_ex * cap), 1)).astype(BF16)
     z_own(send_x, recv_x)
     z_own(send_s, recv_s)
     store(row_place, place_hbm)
 
     g_passed = w_pass(0, full_g, g_direct)
     d_direct = w_start(2, wd_hbm, full_d)
+    s_copies.append(z_start(1, send_s, recv_s, far[0]))
     u_passed = w_pass(1, full_u, u_direct)
+    for copy in x_far:
+        copy.wait_send()
+        copies.remove(copy)
+    s_copies += [z_start(1, send_s, recv_s, k) for k in far[1:]]
     hidden_units = wg_hbm.shape[2]
-    arrived(x_copies)
+    arrived(x_far + x_near)
     arrived(g_passed)
     own[4].wait()
     gate_act = dot(recv_x[...], full_g[...].reshape(width, hidden_units))
@@ -435,7 +436,7 @@
     rows, width = x_rows.shape
     cap = 2 * rows // n_ex
     _, piece, hidden = w_gate.shape
-    if cap % 16 or piece % 32 or hidden % 32 or not power_of_two(n_ex) or n_dp != 4:
+    if cap % 16 or piece % 32 or hidden % 32 or not power_of_two(n_ex) or n_ex < 4 or n_dp != 4:
         return collective_device(x_rows, expert_ids, gates, cotangent, w_gate, w_up, w_down)
     total = n_ex * cap
     hbm = pl.BlockSpec(memory_space=pltpu.HBM)

time: 56.2 us -> 60.1 us (1.069)
  Pallas kernels: 55.4 us -> 59.3 us
    pallas_call x1, Pallas kernels: 53.1 us -> 56.9 us  [per_device(): pl.pallas_call(functools.partial(layer_kernel, n_dp, n_ex, cap), out_shap...]
where the time goes in v6:
time: 60.1 us; the launch traced here: 59.9 us
  Pallas kernels  59.3 us (99%)
  between operations  0.64 us (1%)
    pallas_call x1, Pallas kernels, per_device(): pl.pallas_call(functools.partial(layer_kernel, n_dp, n_ex, cap), out_shap...  56.9 us
    pallas_call x1, Pallas kernels, per_device(): pl.pallas_call(results_kernel, out_shape=(igrad_shape, *shapes), in_specs...  2.38 us

profile of v6, /device:TPU:0, one launch (start us, length us, event | category | flops | bytes accessed | tf_op | source)
XLA Modules:
  0.0 59.9 jit_solution(12468103299151515932)
XLA Ops:
  0.6 56.9 %shard_map.118 = (bf16[128,1024]{1,0:T(8,128)(2,1)}, bf16[256,1024]{1,0:T(8,128)(2,1)}, f32[1,128]{1,0:T(1,128)}, bf16[1,256,384]{2,1,0:T(8,128)(2,1)}, bf16[1,2...) custom-call(bf16[128,1024]{1,0:T(8,128)(2,1)} %x_hbm.1, s32[1,128]{1,0:T(1,128)} %bitcast.3, ...), custom_call_target="tpu_custom_call" | custom-call | tf_op jit(solution)/shard_map/pallas_call | solution.py:461
  57.5 2.4 %shard_map.119 = (bf16[128,1024]{1,0:T(8,128)(2,1)}, bf16[128,1024]{1,0:T(8,128)(2,1)}, f32[1,128]{1,0:T(1,128)}, bf16[1,256,384]{2,1,0:T(8,128)(2,1)}, bf16[1,2...) custom-call(bf16[256,1024]{1,0:T(8,128)(2,1)} %get-tuple-element.19.refs_0_, ...), custom_call_target="tpu_custom_call" | custom-call | tf_op jit(solution)/shard_map/pallas_call | solution.py:490

commit v7 on v6

--- a/solution.py
+++ b/solution.py
@@ -329,12 +329,8 @@
 
     g_passed = w_pass(0, full_g, g_direct)
     d_direct = w_start(2, wd_hbm, full_d)
-    s_copies.append(z_start(1, send_s, recv_s, far[0]))
+    s_copies += [z_start(1, send_s, recv_s, k) for k in far]
     u_passed = w_pass(1, full_u, u_direct)
-    for copy in x_far:
-        copy.wait_send()
-        copies.remove(copy)
-    s_copies += [z_start(1, send_s, recv_s, k) for k in far[1:]]
     hidden_units = wg_hbm.shape[2]
     arrived(x_far + x_near)
     arrived(g_passed)

time: 60.1 us -> 60.1 us (level)
  no operation moved by 1% of the time
where the time goes in v7:
time: 60.1 us; the launch traced here: 59.9 us
  Pallas kernels  59.3 us (99%)
  between operations  0.64 us (1%)
    pallas_call x1, Pallas kernels, per_device(): pl.pallas_call(functools.partial(layer_kernel, n_dp, n_ex, cap), out_shap...  56.9 us
    pallas_call x1, Pallas kernels, per_device(): pl.pallas_call(results_kernel, out_shape=(igrad_shape, *shapes), in_specs...  2.38 us

profile of v7, /device:TPU:0, one launch (start us, length us, event | category | flops | bytes accessed | tf_op | source)
XLA Modules:
  0.0 59.9 jit_solution(8463556015792674643)
XLA Ops:
  0.6 56.9 %shard_map.118 = (bf16[128,1024]{1,0:T(8,128)(2,1)}, bf16[256,1024]{1,0:T(8,128)(2,1)}, f32[1,128]{1,0:T(1,128)}, bf16[1,256,384]{2,1,0:T(8,128)(2,1)}, bf16[1,2...) custom-call(bf16[128,1024]{1,0:T(8,128)(2,1)} %x_hbm.1, s32[1,128]{1,0:T(1,128)} %bitcast.3, ...), custom_call_target="tpu_custom_call" | custom-call | tf_op jit(solution)/shard_map/pallas_call | solution.py:457
  57.5 2.4 %shard_map.119 = (bf16[128,1024]{1,0:T(8,128)(2,1)}, bf16[128,1024]{1,0:T(8,128)(2,1)}, f32[1,128]{1,0:T(1,128)}, bf16[1,256,384]{2,1,0:T(8,128)(2,1)}, bf16[1,2...) custom-call(bf16[256,1024]{1,0:T(8,128)(2,1)} %get-tuple-element.19.refs_0_, ...), custom_call_target="tpu_custom_call" | custom-call | tf_op jit(solution)/shard_map/pallas_call | solution.py:486
